TPU v7x, 512 devices: a whole 4x8x8 slice. The times are simulated.
512 devices in a mesh: dp: 32 (over x, y), tensor: 16 (over z, core).
Axes of the slice: x: 4, y: 8, z: 8, core: 2. Of those that a mesh axis runs over, the one named last changes fastest.
Arguments:
- gate_pre: bfloat16 [2, 4096, 53248], P(None, 'dp', 'tensor'), parts along dimension 1, may hold values from -8 to 8
- up_pre: bfloat16 [2, 4096, 53248], P(None, 'dp', 'tensor'), parts along dimension 1, may hold values from -8 to 8
- rotation52: bfloat16 [52, 52], replicated, may hold values from -0.875 to 0.875
Outputs:
- quantized: bfloat16 [2, 4096, 53248], P(None, 'dp', 'tensor'), parts along dimension 1
- peaks: float32 [2, 4096], P(None, 'dp'), parts along dimension 1
There are 32 independent parts, one for each index of `dp`. A program takes and returns all parts, laid end to end along the dimension named above; an argument that names none is the same for every part. Nothing has to cross between parts.
All inputs are finite; a program needn't handle non-finite values. Where the computation divides by a largest or mean magnitude, that divisor is 1e-20 or more.
Results may differ from a plain program's by a relative error of at most 0.005.
Values may be sent and summed in bfloat16 or wider, within the bound.
No kernel may reach another device: no remote copies, remote signals or barrier semaphores. Data moves between devices by JAX's collectives and lax.ppermute only.
A program may use at most 128 MiB of HBM per device.

v0:
```python
import jax
import jax.numpy as jnp
from jax import lax
from jax.sharding import PartitionSpec as P

HAD_BIG = 1024


def swapped(value, axis, distance):
    mask = 2**distance
    pairs = [(source, source ^ mask) for source in range(lax.axis_size(axis))]
    return lax.ppermute(value, axis, pairs)


def sylvester(order):
    index = jnp.arange(order, dtype=jnp.int32)
    parity = jnp.zeros((order, order), jnp.int32)
    for level in range(order.bit_length() - 1):
        parity = parity + jnp.right_shift(index[:, None], level) % 2 * (
            jnp.right_shift(index[None, :], level) % 2
        )
    return (1 - 2 * (parity % 2)).astype(jnp.float32)


def kron_hadamard(mixed, order):
    bits = order.bit_length() - 1
    high = 2 ** (bits // 2)
    low = order // high
    steps, rows, _, cols = mixed.shape
    split = mixed.reshape(steps, rows, high, low, cols)
    split = jnp.einsum("srhlc,hk->srklc", split, sylvester(high), precision=lax.Precision.HIGHEST)
    split = jnp.einsum("srklc,lm->srkmc", split, sylvester(low), precision=lax.Precision.HIGHEST)
    return split.reshape(steps, rows, order, cols)


def body(gate_pre, up_pre, rotation52):
    small = rotation52.shape[0]
    width = gate_pre.shape[2]
    hidden = (jax.nn.silu(gate_pre.astype(jnp.float32)) * up_pre.astype(jnp.float32)).astype(
        jnp.bfloat16
    )
    steps, rows = (hidden.shape[0], hidden.shape[1])
    local_big = width // small
    blocks = hidden.reshape(steps, rows, local_big, small)
    mixed = jnp.einsum("srba,ac->srbc", blocks, rotation52, preferred_element_type=jnp.float32)
    current = kron_hadamard(mixed, local_big)
    position = lax.axis_index("tensor")
    for level in range(lax.axis_size("tensor").bit_length() - 1):
        partner = swapped(current, "tensor", level)
        upper = jnp.right_shift(position, level) % 2
        current = jnp.where(upper == 0, current + partner, partner - current)
    rotated = current * HAD_BIG ** (-0.5)
    local_peak = jnp.max(jnp.abs(rotated), axis=(2, 3))
    peaks = lax.pmax(local_peak, "tensor") + 1e-06
    quantized = (rotated / peaks[:, :, None, None]).astype(jnp.bfloat16).reshape(steps, rows, width)
    return (quantized, peaks)


def solution(mesh):
    in_specs = (P(None, "dp", "tensor"), P(None, "dp", "tensor"), P())
    out_specs = (P(None, "dp", "tensor"), P(None, "dp"))
    return jax.shard_map(body, mesh=mesh, in_specs=in_specs, out_specs=out_specs, check_vma=False)
```

profile of v0, /device:TPU:1, one launch (start us, length us, event | category | flops | bytes accessed | tf_op | source)
XLA Modules:
  0.0 461.7 jit_solution(15784555476004495894)
XLA Ops:
  0.6 0.0 copy-start
  0.7 3.0 fusion.8
  3.7 1.9 copy.17
  5.6 0.0 copy-done
  5.6 0.7 fusion.15
  6.3 5.0 %fusion.9 = f32[2,128,8,8,52]{1,2,4,3,0:T(8,128)S(1)} fusion(f32[2,128,8,8,52]{1,4,3,2,0:T(8,128)S(1)} %fusion.15, s32[8]{0:T(128)S(1)} %get-tuple-element.8, s32[8]{0:T(128)S(1)} %get-tuple-element.9, s32[8]{0:T(128)S(1)} %and_select_fusion.2), kind=kOutput, calls=%fused_computation.18 | convolution fusion | flops 81790144 | bytes 6815840 | tf_op jit(solution)/shard_map/srhlc,hk->srklc/dot_general | solution.py:31
  11.3 4.7 %fusion.12 = f32[2,128,8,8,52]{1,3,4,2,0:T(8,128)S(1)} fusion(f32[2,128,8,8,52]{1,2,4,3,0:T(8,128)S(1)} %fusion.9, s32[8]{0:T(128)S(1)} %get-tuple-element.8, s32[8]{0:T(128)S(1)} %get-tuple-element.9, s32[8]{0:T(128)S(1)} %and_select_fusion.2), kind=kOutput, calls=%fused_computation.19 | convolution fusion | flops 81790144 | bytes 6815840 | tf_op jit(solution)/shard_map/srklc,lm->srkmc/dot_general | solution.py:32
  16.0 2.2 copy.41
  18.2 9.0 %collective-permute-start = (f32[2,128,64,52]{1,2,3,0:T(8,128)}, f32[2,128,64,52]{1,2,3,0:T(8,128)}, u32[]{:S(2)}, u32[]{:S(2)}) collective-permute-start(f32[2,128,64,52]{1,2,3,0:T(8,128)} %bitcast.19), channel_id=1, source_target_pairs={{0,1},{1,0},{2,3},{3,2},{4,5},{5,4},{6,7},{7,6},{8,9},{9,8},{10,11... | collective-permute-start | bytes 10223624 | tf_op jit(solution)/shard_map/ppermute | solution.py:12
  27.2 5.8 %collective-permute-done = f32[2,128,64,52]{1,2,3,0:T(8,128)} collective-permute-done((f32[2,128,64,52]{1,2,3,0:T(8,128)}, f32[2,128,64,52]{1,2,3,0:T(8,128)}, u32[]{:S(2)}, u32[]{:S(2)}) %collective-permute-start) | collective-permute-done | bytes 3407904 | tf_op jit(solution)/shard_map/ppermute | solution.py:12
  33.0 4.6 subtract_select_fusion.2
  37.5 1.9 collective-permute-start.1
  39.5 75.2 %collective-permute-done.1 = f32[2,128,64,52]{1,2,3,0:T(8,128)} collective-permute-done((f32[2,128,64,52]{1,2,3,0:T(8,128)}, f32[2,128,64,52]{1,2,3,0:T(8,128)}, u32[]{:S(2)}, u32[]{:S(2)}) %collective-permute-start.1) | collective-permute-done | bytes 3407904 | tf_op jit(solution)/shard_map/ppermute | solution.py:12
  114.7 3.8 subtract_select_fusion.1
  118.5 1.9 collective-permute-start.2
  120.4 149.6 %collective-permute-done.2 = f32[2,128,64,52]{1,2,3,0:T(8,128)} collective-permute-done((f32[2,128,64,52]{1,2,3,0:T(8,128)S(1)}, f32[2,128,64,52]{1,2,3,0:T(8,128)}, u32[]{:S(2)}, u32[]{:S(2)}) %collective-permute-start.2) | collective-permute-done | bytes 3407904 | tf_op jit(solution)/shard_map/ppermute | solution.py:12
  270.0 3.8 subtract_select_fusion
  273.8 4.4 collective-permute-start.3
  278.1 149.4 %collective-permute-done.3 = f32[2,128,64,52]{1,2,3,0:T(8,128)} collective-permute-done((f32[2,128,64,52]{1,2,3,0:T(8,128)S(1)}, f32[2,128,64,52]{1,2,3,0:T(8,128)}, u32[]{:S(2)}, u32[]{:S(2)}) %collective-permute-start.3) | collective-permute-done | bytes 3407904 | tf_op jit(solution)/shard_map/ppermute | solution.py:12
  427.6 2.5 abs_reduce_fusion
  430.1 23.4 %pmax.7 = f32[2,128]{1,0:T(2,128)S(1)} all-reduce(f32[2,128]{1,0:T(2,128)S(1)} %abs_reduce_fusion), channel_id=1, replica_groups=mesh['dp'=32,'tensor'=16] {'tensor'}, use_global_device_ids=true, to_apply=%region_1.2 | all-reduce | flops 256 | bytes 2048 | tf_op jit(solution)/shard_map/pmax | solution.py:54
  453.5 2.8 divide_convert_fusion
  456.3 1.8 copy.23
  458.1 3.6 copy.24
  (7 shorter events, 0.0 us)
Async XLA Ops:
  0.6 5.0 %copy-start = (bf16[52,52]{1,0:T(8,128)(2,1)S(1)}, bf16[52,52]{1,0:T(8,128)(2,1)}, u32[]{:S(2)}) copy-start(bf16[52,52]{1,0:T(8,128)(2,1)} %param.5) | copy-start | bytes 16228
  18.2 14.8 %collective-permute-start = (f32[2,128,64,52]{1,2,3,0:T(8,128)}, f32[2,128,64,52]{1,2,3,0:T(8,128)}, u32[]{:S(2)}, u32[]{:S(2)}) collective-permute-start(f32[2,128,64,52]{1,2,3,0:T(8,128)} %bitcast.19), channel_id=1, source_target_pairs={{0,1},{1,0},{2,3},{3,2},{4,5},{5,4},{6,7},{7,6},{8,9},{9,8},{10,11... | collective-permute-start | bytes 10223624 | tf_op jit(solution)/shard_map/ppermute | solution.py:12
  37.5 77.1 %collective-permute-start.1 = (f32[2,128,64,52]{1,2,3,0:T(8,128)}, f32[2,128,64,52]{1,2,3,0:T(8,128)}, u32[]{:S(2)}, u32[]{:S(2)}) collective-permute-start(f32[2,128,64,52]{1,2,3,0:T(8,128)} %subtract_select_fusion.2), channel_id=1, source_target_pairs={{0,2},{1,3},{2,0},{3,1},{4,6},{5,7},{6,4},{7,5},{8,10},{9,11},{10,... | collective-permute-start | bytes 10223624 | tf_op jit(solution)/shard_map/ppermute | solution.py:12
  118.5 2.0 copy-start.1
  118.5 151.5 %collective-permute-start.2 = (f32[2,128,64,52]{1,2,3,0:T(8,128)S(1)}, f32[2,128,64,52]{1,2,3,0:T(8,128)}, u32[]{:S(2)}, u32[]{:S(2)}) collective-permute-start(f32[2,128,64,52]{1,2,3,0:T(8,128)S(1)} %subtract_select_fusion.1), channel_id=1, source_target_pairs={{0,4},{1,5},{2,6},{3,7},{4,0},{5,1},{6,2},{7,3},{8,12},{9,13},{10,... | collective-permute-start | bytes 10223624 | tf_op jit(solution)/shard_map/ppermute | solution.py:12
  273.8 153.8 %collective-permute-start.3 = (f32[2,128,64,52]{1,2,3,0:T(8,128)S(1)}, f32[2,128,64,52]{1,2,3,0:T(8,128)}, u32[]{:S(2)}, u32[]{:S(2)}) collective-permute-start(f32[2,128,64,52]{1,2,3,0:T(8,128)S(1)} %subtract_select_fusion), channel_id=1, source_target_pairs={{0,8},{1,9},{2,10},{3,11},{4,12},{5,13},{6,14},{7,15},{8,0},{9,1},... | collective-permute-start | bytes 10223624 | tf_op jit(solution)/shard_map/ppermute | solution.py:12
  453.5 2.8 copy-start.2
where the time goes:
time: 462 us
  waiting for transfers between devices  380 us (82%)
  blocking collectives  23.4 us (5%)
  other arithmetic  20.4 us (4%)
  starting transfers between devices  17.1 us (4%)
  matrix products  10.3 us (2%)
  local copies, waits for them, and re-layouts  9.55 us (2%)
    ppermute x4, waiting for transfers between devices, swapped(): return lax.ppermute(value, axis, pairs)  380 us
    pmax x1, blocking collectives, body(): peaks = lax.pmax(local_peak, 'tensor') + 1e-06  23.4 us
    ppermute x4, starting transfers between devices, swapped(): return lax.ppermute(value, axis, pairs)  17.1 us
    select_n x3, other arithmetic, body(): current = jnp.where(upper == 0, current + partner, partner - current)  12.1 us
  transfers between devices with their start and end apart: 4, of which 4 were waited for; matrix products, arithmetic and copies ran while one was open for 0% of the time, Pallas kernels for 0%

commit v1 on v0

v1 whole, which is shorter than its diff:
```python
import jax
import jax.numpy as jnp
from jax import lax
from jax.experimental import pallas as pl
from jax.experimental.pallas import tpu as pltpu
from jax.sharding import PartitionSpec as P

HAD_BIG = 1024
LOW = 32
LANES = 128
VMEM_LIMIT = 48 * 1024 * 1024


def parity_sign(left, right):
    both = left & right
    parity = both
    for level in (1, 2, 3, 4):
        parity = parity ^ (both >> level)
    return 1 - 2 * (parity & 1)


def factor_kernel(rotation_ref, out_ref):
    small = rotation_ref.shape[0]
    width = out_ref.shape[0]
    f32, bf16 = jnp.float32, jnp.bfloat16

    def expand(rows, shape, offset, dim):
        index = lax.broadcasted_iota(jnp.int32, shape, dim) + offset
        other = lax.broadcasted_iota(jnp.int32, shape, 1 - dim)
        block = (index * 1261) >> 16
        value = block if rows else index - block * small
        return (value == other).astype(f32).astype(bf16)

    tiled = jnp.dot(
        rotation_ref[...], expand(False, (small, width), 0, 1), preferred_element_type=f32
    ).astype(bf16)
    big = lax.broadcasted_iota(jnp.int32, (LOW, width), 0)
    lane = lax.broadcasted_iota(jnp.int32, (LOW, width), 1)
    signs = parity_sign(big, (lane * 1261) >> 16).astype(f32).astype(bf16)

    @pl.loop(0, width // LANES)
    def _(step):
        start = pl.multiple_of(step * LANES, LANES)
        value = jnp.dot(expand(False, (LANES, small), start, 0), tiled, preferred_element_type=f32)
        sign = jnp.dot(expand(True, (LANES, LOW), start, 0), signs, preferred_element_type=f32)
        out_ref[pl.ds(start, LANES), :] = (value * sign).astype(bf16)


def factor(rotation52):
    width = LOW * rotation52.shape[0]
    return pl.pallas_call(
        factor_kernel,
        out_shape=jax.ShapeDtypeStruct((width, width), jnp.bfloat16),
        in_specs=[pl.BlockSpec(memory_space=pltpu.VMEM)],
        out_specs=pl.BlockSpec(memory_space=pltpu.VMEM),
        compiler_params=pltpu.CompilerParams(vmem_limit_bytes=VMEM_LIMIT),
        cost_estimate=pl.CostEstimate(
            flops=2 * width * width * 84, bytes_accessed=2 * width * width, transcendentals=0
        ),
        name="kron_factor",
    )(rotation52)


def butterfly(values):
    count = len(values)
    distance = 1
    while distance < count:
        values = [
            values[i] + values[i ^ distance] if i & distance == 0 else values[i ^ distance] - values[i]
            for i in range(count)
        ]
        distance *= 2
    return values


def transform_kernel(hidden_ref, factor_ref, out_ref, product_ref, rotated_ref):
    groups, rows, width = hidden_ref.shape
    low = factor_ref.shape[0]
    halves = width // low
    f32 = jnp.float32
    peak = [jnp.zeros((8, LANES), f32) for _ in range(rows // 8)]
    for start in range(0, low, 2 * LANES):
        span = min(2 * LANES, low - start)
        for half in range(halves):
            product_ref[half, :, :, :span] = jnp.dot(
                hidden_ref[:, :, half * low : (half + 1) * low].reshape(groups * rows, low),
                factor_ref[:, start : start + span],
                preferred_element_type=f32,
            ).reshape(groups, rows, span)
        for part in range(rows // 8):
            at = slice(part * 8, part * 8 + 8)
            for lane in range(0, span, LANES):
                values = butterfly(
                    [
                        product_ref[half, group, at, lane : lane + LANES]
                        for group in range(groups)
                        for half in range(halves)
                    ]
                )
                for i, value in enumerate(values):
                    group, half = divmod(i, halves)
                    column = half * low + start + lane
                    rotated_ref[group, at, column : column + LANES] = value
                    peak[part] = jnp.maximum(peak[part], jnp.abs(value))
    scale = HAD_BIG**-0.5
    largest = jnp.concatenate([jnp.max(p, axis=1, keepdims=True) for p in peak], axis=0)
    largest = largest * scale + 1e-6
    inverse = scale / largest
    coarse = largest.astype(jnp.bfloat16).astype(f32)
    lanes = lax.broadcasted_iota(jnp.int32, (rows, LANES), 1)
    parts = jnp.where(lanes == 0, coarse, largest - coarse).astype(jnp.bfloat16)
    for group in range(groups):
        out_ref[group, :, :width] = (rotated_ref[group] * inverse).astype(out_ref.dtype)
        out_ref[group, :, width:] = parts


def transform(hidden, weights):
    groups, rows, width = hidden.shape
    low = weights.shape[0]
    return pl.pallas_call(
        transform_kernel,
        out_shape=jax.ShapeDtypeStruct((groups, rows, width + LANES), jnp.bfloat16),
        in_specs=[pl.BlockSpec(memory_space=pltpu.VMEM)] * 2,
        out_specs=pl.BlockSpec(memory_space=pltpu.VMEM),
        scratch_shapes=[
            pltpu.VMEM((width // low, groups, rows, 2 * LANES), jnp.float32),
            pltpu.VMEM((groups, rows, width), jnp.float32),
        ],
        compiler_params=pltpu.CompilerParams(vmem_limit_bytes=VMEM_LIMIT),
        cost_estimate=pl.CostEstimate(
            flops=2 * groups * rows * width * low,
            bytes_accessed=4 * groups * rows * width + 2 * low * low,
            transcendentals=0,
        ),
        name="rotate_rows",
    )(hidden, weights)


def body(gate_pre, up_pre, rotation52):
    steps, rows, width = gate_pre.shape
    groups = lax.axis_size("tensor")
    f32 = jnp.float32
    weights = factor(rotation52)
    hidden = (jax.nn.silu(gate_pre.astype(f32)) * up_pre.astype(f32)).astype(jnp.bfloat16)
    hidden = hidden.reshape(groups, steps * rows // groups, width)
    mine = lax.all_to_all(hidden, "tensor", 0, 0)
    packed = lax.all_to_all(transform(mine, weights), "tensor", 0, 0)
    quantized = packed[:, :, :width].reshape(steps, rows, width)
    peaks = packed[:, :, width].astype(f32) + packed[:, :, width + 1].astype(f32)
    return (quantized, peaks.reshape(steps, rows))


def solution(mesh):
    in_specs = (P(None, "dp", "tensor"), P(None, "dp", "tensor"), P())
    out_specs = (P(None, "dp", "tensor"), P(None, "dp"))
    return jax.shard_map(body, mesh=mesh, in_specs=in_specs, out_specs=out_specs, check_vma=False)
```

time: 462 us -> 115 us (0.25)
  waiting for transfers between devices: 380 us -> 33.6 us
  blocking collectives: 23.4 us -> 48.2 us
  other arithmetic: 20.4 us -> 4.34 us
  Pallas kernels: 0 us -> 11.5 us
  matrix products: 10.3 us -> 0 us
  local copies, waits for them, and re-layouts: 9.55 us -> 4.33 us
  starting transfers between devices: 17.1 us -> 12 us
    ppermute x4 -> x0, waiting for transfers between devices: 380 us -> none  [swapped(): return lax.ppermute(value, axis, pairs)]
    all_to_all x0 -> x1, blocking collectives: none -> 48.2 us  [body(): packed = lax.all_to_all(transform(mine, weights), 'tensor', 0, 0)]
    all_to_all x0 -> x1, waiting for transfers between devices: none -> 33.6 us  [body(): mine = lax.all_to_all(hidden, 'tensor', 0, 0)]
    pmax x1 -> x0, blocking collectives: 23.4 us -> none  [body(): peaks = lax.pmax(local_peak, 'tensor') + 1e-06]
    ppermute x4 -> x0, starting transfers between devices: 17.1 us -> none  [swapped(): return lax.ppermute(value, axis, pairs)]
    select_n x5 -> x0, other arithmetic: 12.1 us -> none  [the longest x3 12.1 us: body(): current = jnp.where(upper == 0, current + partner, partner - current)]
    all_to_all x0 -> x1, starting transfers between devices: none -> 12 us  [body(): mine = lax.all_to_all(hidden, 'tensor', 0, 0)]
    pallas_call x0 -> x2, Pallas kernels: none -> 11.5 us  [the longest x1 6.48 us: transform(): pl.pallas_call(transform_kernel, out_shape=jax.ShapeDtypeStruct((groups,...]
  transfers between devices with their start and end apart: 4 -> 1, of which waited for: 4 -> 1; matrix products, arithmetic and copies ran while one was open for 0% -> 0% of each run, Pallas kernels for 0% -> 4%
where the time goes in v1:
time: 115 us
  blocking collectives  48.2 us (42%)
  waiting for transfers between devices  33.6 us (29%)
  starting transfers between devices  12 us (10%)
  Pallas kernels  11.5 us (10%)
  other arithmetic  4.34 us (4%)
  local copies, waits for them, and re-layouts  4.33 us (4%)
    all_to_all x1, blocking collectives, body(): packed = lax.all_to_all(transform(mine, weights), 'tensor', 0, 0)  48.2 us
    all_to_all x1, waiting for transfers between devices, body(): mine = lax.all_to_all(hidden, 'tensor', 0, 0)  33.6 us
    all_to_all x1, starting transfers between devices, body(): mine = lax.all_to_all(hidden, 'tensor', 0, 0)  12 us
    pallas_call x1, Pallas kernels, transform(): pl.pallas_call(transform_kernel, out_shape=jax.ShapeDtypeStruct((groups,...  6.48 us
    pallas_call x1, Pallas kernels, factor(): pl.pallas_call(factor_kernel, out_shape=jax.ShapeDtypeStruct((width, widt...  5.07 us
    convert_element_type x1, other arithmetic, body(): (jax.nn.silu(gate_pre.astype(f32)) * up_pre.astype(f32)).astype(jnp.bfloa...  4.16 us
    unnamed x4, local copies, waits for them, and re-layouts  2.39 us
  transfers between devices with their start and end apart: 1, of which 1 were waited for; matrix products, arithmetic and copies ran while one was open for 0% of the time, Pallas kernels for 4%

profile of v1, /device:TPU:1, one launch (start us, length us, event | category | flops | bytes accessed | tf_op | source)
XLA Modules:
  0.0 114.7 jit_solution(9654295788165785772)
XLA Ops:
  0.6 4.2 %fusion.4 = bf16[2,128,3328]{2,1,0:T(8,128)(2,1)} fusion(bf16[2,128,3328]{2,1,0:T(8,128)(2,1)} %param.4, bf16[2,128,3328]{2,1,0:T(8,128)(2,1)} %param.3), kind=kLoop, calls=%fused_computation.6 | loop fusion | flops 6815744 | bytes 5111808 | tf_op jit(solution)/shard_map/convert_element_type | solution.py:144
  4.8 0.0 copy-start.1
  4.8 12.0 %all-to-all-start = ((bf16[16,16,3328]{2,1,0:T(8,128)(2,1)}), bf16[16,16,3328]{2,1,0:T(8,128)(2,1)S(1)}, u32[]{:S(2)}, u32[]{:S(2)}) async-start(bf16[16,16,3328]{2,1,0:T(8,128)(2,1)} %bitcast), calls=%async_computation | async-start | bytes 3407872 | tf_op jit(solution)/shard_map/all_to_all | solution.py:146
  16.8 0.0 copy-done.1
  16.8 5.1 %kron_factor.1.factor_ref = bf16[1664,1664]{1,0:T(8,128)(2,1)S(1)} custom-call(bf16[52,52]{1,0:T(8,128)(2,1)S(1)} %copy-done.1), custom_call_target="tpu_custom_call" | custom-call | flops 465174528 | bytes 5537792 | tf_op jit(solution)/shard_map/kron_factor/pallas_call | solution.py:51
  21.8 0.0 copy-start
  21.8 2.4 %copy-done = bf16[1664,1664]{1,0:T(8,128)(2,1)} copy-done((bf16[1664,1664]{1,0:T(8,128)(2,1)}, bf16[1664,1664]{1,0:T(8,128)(2,1)S(1)}, u32[]{:S(2)}) %copy-start) | copy-done | bytes 5537816
  24.2 33.6 %all-to-all-done.hidden_ref = bf16[16,16,3328]{2,1,0:T(8,128)(2,1)S(1)} async-done(((bf16[16,16,3328]{2,1,0:T(8,128)(2,1)}), bf16[16,16,3328]{2,1,0:T(8,128)(2,1)S(1)}, u32[]{:S(2)}, u32[]{:S(2)}) %all-to-all-start) | async-done | bytes 1703968 | tf_op jit(solution)/shard_map/all_to_all | solution.py:146
  57.8 6.5 %rotate_rows.1 = bf16[16,16,3456]{2,1,0:T(8,128)(2,1)S(1)} custom-call(bf16[16,16,3328]{2,1,0:T(8,128)(2,1)S(1)} %all-to-all-done.hidden_ref, bf16[1664,1664]{1,0:T(8,128)(2,1)} %copy-done), custom_call_target="tpu_custom_call" | custom-call | flops 2835349504 | bytes 8945664 | tf_op jit(solution)/shard_map/rotate_rows/pallas_call | solution.py:120
  64.3 48.2 %all_to_all.10 = bf16[16,16,3456]{2,1,0:T(8,128)(2,1)S(1)} all-to-all(bf16[16,16,3456]{2,1,0:T(8,128)(2,1)S(1)} %rotate_rows.1), channel_id=1, replica_groups=mesh['dp'=32,'tensor'=16] {'tensor'}, dimensions={0} | all-to-all | bytes 3538944 | tf_op jit(solution)/shard_map/all_to_all | solution.py:147
  112.5 0.2 add_reduce_fusion
  112.7 0.6 add.13
  113.4 1.3 %slice.12 = bf16[16,16,3328]{2,1,0:T(8,128)(2,1)} slice(bf16[16,16,3456]{2,1,0:T(8,128)(2,1)S(1)} %all_to_all.10), slice={[0:16], [0:16], [0:3328]} | slice | bytes 3407872 | tf_op jit(solution)/shard_map/slice | solution.py:148
Async XLA Ops:
  4.8 12.0 %copy-start.1 = (bf16[52,52]{1,0:T(8,128)(2,1)S(1)}, bf16[52,52]{1,0:T(8,128)(2,1)}, u32[]{:S(2)}) copy-start(bf16[52,52]{1,0:T(8,128)(2,1)} %rotation_ref.1) | copy-start | bytes 16228
  4.8 53.0 %all-to-all-start = ((bf16[16,16,3328]{2,1,0:T(8,128)(2,1)}), bf16[16,16,3328]{2,1,0:T(8,128)(2,1)S(1)}, u32[]{:S(2)}, u32[]{:S(2)}) async-start(bf16[16,16,3328]{2,1,0:T(8,128)(2,1)} %bitcast), calls=%async_computation | async-start | bytes 3407872 | tf_op jit(solution)/shard_map/all_to_all | solution.py:146
  21.8 2.4 %copy-start = (bf16[1664,1664]{1,0:T(8,128)(2,1)}, bf16[1664,1664]{1,0:T(8,128)(2,1)S(1)}, u32[]{:S(2)}) copy-start(bf16[1664,1664]{1,0:T(8,128)(2,1)S(1)} %kron_factor.1.factor_ref) | copy-start | bytes 16613380

commit v2 on v1

v2 whole, which is shorter than its diff:
```python
import jax
import jax.numpy as jnp
from jax import lax
from jax.experimental import pallas as pl
from jax.experimental.pallas import tpu as pltpu
from jax.sharding import PartitionSpec as P

HAD_BIG = 1024
LOW = 32
LANES = 128
TILE = 2 * LANES
VMEM_LIMIT = 20 * 1024 * 1024
STREAM_LIMIT = 58 * 1024 * 1024


def hidden_kernel(gate_hbm, up_hbm, out_ref, gate_ref, up_ref, sems):
    chunks, rows, width = gate_ref.shape
    f32 = jnp.float32
    copies = []
    for chunk in range(chunks):
        at = pl.ds(chunk * rows, rows)
        for k, (source, target) in enumerate(((gate_hbm, gate_ref), (up_hbm, up_ref))):
            copy = pltpu.make_async_copy(source.at[at], target.at[chunk], sems.at[chunk, k])
            copy.start()
            copies.append(copy)
    for chunk in range(chunks):
        copies[2 * chunk].wait()
        copies[2 * chunk + 1].wait()

        @pl.loop(0, rows // 16)
        def _(step):
            at = pl.ds(pl.multiple_of(step * 16, 16), 16)
            gate = gate_ref[chunk, at].astype(f32)
            half = 0.5 * gate
            silu = half * jnp.tanh(half) + half
            value = (silu * up_ref[chunk, at].astype(f32)).astype(out_ref.dtype)
            out_ref[pl.ds(pl.multiple_of(chunk * rows + step * 16, 16), 16), :] = value


def gated(gate, up):
    rows, width = gate.shape
    chunks = 4
    held = pltpu.VMEM((chunks, rows // chunks, width), gate.dtype)
    return pl.pallas_call(
        hidden_kernel,
        out_shape=jax.ShapeDtypeStruct(gate.shape, gate.dtype),
        in_specs=[pl.BlockSpec(memory_space=pl.ANY)] * 2,
        out_specs=pl.BlockSpec(memory_space=pltpu.VMEM),
        scratch_shapes=[held, held, pltpu.SemaphoreType.DMA((chunks, 2))],
        compiler_params=pltpu.CompilerParams(vmem_limit_bytes=STREAM_LIMIT),
        cost_estimate=pl.CostEstimate(
            flops=6 * rows * width, bytes_accessed=6 * rows * width, transcendentals=rows * width
        ),
        name="gated_hidden",
    )(gate, up)


def unpack_kernel(packed_ref, out_hbm, peak_ref, sem):
    groups, rows, packed = packed_ref.shape
    width = out_hbm.shape[2]
    steps, span = peak_ref.shape
    per = groups // steps
    copies = []
    count = sem.shape[0]
    for part in range(count):
        at = pl.ds(part * (groups // count), groups // count)
        copy = pltpu.make_async_copy(
            packed_ref.at[at, :, pl.ds(0, width)], out_hbm.at[at], sem.at[part]
        )
        copy.start()
        copies.append(copy)
    lanes = lax.broadcasted_iota(jnp.int32, (8, packed - width), 1)
    both = (lanes < 2).astype(jnp.float32).astype(jnp.bfloat16)
    for step in range(steps):
        parts = packed_ref[step * per : step * per + per, :, width:].reshape(span, packed - width)
        sums = lax.dot_general(
            both, parts, (((1,), (1,)), ((), ())), preferred_element_type=jnp.float32
        )
        peak_ref[step : step + 1, :] = sums[:1]
    for copy in copies:
        copy.wait()


def unpack(packed, steps, span, width):
    quantized, peaks = pl.pallas_call(
        unpack_kernel,
        out_shape=(
            jax.ShapeDtypeStruct((*packed.shape[:2], width), packed.dtype),
            jax.ShapeDtypeStruct((steps, span), jnp.float32),
        ),
        in_specs=[pl.BlockSpec(memory_space=pltpu.VMEM)],
        out_specs=(pl.BlockSpec(memory_space=pl.ANY), pl.BlockSpec(memory_space=pltpu.VMEM)),
        scratch_shapes=[pltpu.SemaphoreType.DMA((4,))],
        compiler_params=pltpu.CompilerParams(vmem_limit_bytes=VMEM_LIMIT),
        name="unpack",
    )(packed)
    return quantized.reshape(steps, span, width), peaks


def parity_sign(left, right):
    both = left & right
    parity = both
    for level in (1, 2, 3, 4):
        parity = parity ^ (both >> level)
    return 1 - 2 * (parity & 1)


def factor_kernel(rotation_ref, base_ref, sign_ref):
    small = rotation_ref.shape[0]
    height, width = base_ref.shape
    f32, bf16 = jnp.float32, jnp.bfloat16

    def block(index):
        return (index * 1261) >> 16

    def iota(shape, dim):
        return lax.broadcasted_iota(jnp.int32, shape, dim)

    def one_where(mask):
        return mask.astype(f32).astype(bf16)

    lane = iota((small, width), 1)
    across = one_where(lane - block(lane) * small == iota((small, width), 0))
    tiled = jnp.dot(rotation_ref[...], across, preferred_element_type=f32).astype(bf16)
    row = iota((height, small), 0)
    down = one_where(row - block(row) * small == iota((height, small), 1))
    value = jnp.dot(down, tiled, preferred_element_type=f32)
    shape = (height, width)
    sign = parity_sign(block(iota(shape, 0)), block(iota(shape, 1))).astype(f32)
    base_ref[...] = (value * sign).astype(bf16)
    shape = sign_ref.shape
    sign_ref[...] = parity_sign(4 * iota(shape, 0), block(iota(shape, 1))).astype(f32).astype(bf16)


def factor(rotation52):
    small = rotation52.shape[0]
    width = LOW * small
    return pl.pallas_call(
        factor_kernel,
        out_shape=(
            jax.ShapeDtypeStruct((4 * small, width), jnp.bfloat16),
            jax.ShapeDtypeStruct((16, width), jnp.bfloat16),
        ),
        in_specs=[pl.BlockSpec(memory_space=pltpu.VMEM)],
        out_specs=[pl.BlockSpec(memory_space=pltpu.VMEM)] * 2,
        compiler_params=pltpu.CompilerParams(vmem_limit_bytes=VMEM_LIMIT),
        cost_estimate=pl.CostEstimate(
            flops=2 * 4 * small * width * 52, bytes_accessed=8 * small * width, transcendentals=0
        ),
        name="kron_factor",
    )(rotation52)


def butterfly(values):
    count = len(values)
    distance = 1
    while distance < count:
        values = [
            values[i] + values[i ^ distance] if i & distance == 0 else values[i ^ distance] - values[i]
            for i in range(count)
        ]
        distance *= 2
    return values


def transform_kernel(hidden_ref, base_ref, sign_ref, out_ref, factor_ref, product_ref, rotated_ref):
    groups, rows, width = hidden_ref.shape
    height, low = base_ref.shape
    halves = width // low
    f32 = jnp.float32
    starts = list(range(0, low, TILE))
    peak = [jnp.zeros((8, LANES), f32) for _ in range(rows // 8)]

    def expand(n):
        size = min(TILE, low - starts[n])
        at = slice(starts[n], starts[n] + size)
        for i in range(low // height):
            factor_ref[n % 2, i * height : (i + 1) * height, :size] = (
                base_ref[:, at] * sign_ref[i : i + 1, at]
            )

    def multiply(n):
        size = min(TILE, low - starts[n])
        for half in range(halves):
            product_ref[n % 2, half, :, :, :size] = jnp.dot(
                hidden_ref[:, :, half * low : (half + 1) * low].reshape(groups * rows, low),
                factor_ref[n % 2, :, :size],
                preferred_element_type=f32,
            ).reshape(groups, rows, size)

    def combine(n):
        for part in range(rows // 8):
            at = slice(part * 8, part * 8 + 8)
            for lane in range(0, min(TILE, low - starts[n]), LANES):
                values = butterfly(
                    [
                        product_ref[n % 2, half, group, at, lane : lane + LANES]
                        for group in range(groups)
                        for half in range(halves)
                    ]
                )
                for i, value in enumerate(values):
                    group, half = divmod(i, halves)
                    column = half * low + starts[n] + lane
                    rotated_ref[group, at, column : column + LANES] = value
                sizes = [jnp.abs(value) for value in values] + [peak[part]]
                while len(sizes) > 1:
                    sizes = [jnp.maximum(*sizes[:2])] + sizes[2:]
                peak[part] = sizes[0]

    expand(0)
    for n in range(len(starts)):
        if n + 1 < len(starts):
            expand(n + 1)
        multiply(n)
        if n > 0:
            combine(n - 1)
    combine(len(starts) - 1)
    scale = HAD_BIG**-0.5
    largest = jnp.concatenate([jnp.max(p, axis=1, keepdims=True) for p in peak], axis=0)
    largest = largest * scale + 1e-6
    inverse = scale / largest
    coarse = largest.astype(jnp.bfloat16).astype(f32)
    lanes = lax.broadcasted_iota(jnp.int32, (rows, LANES), 1)
    parts = jnp.where(lanes == 0, coarse, jnp.where(lanes == 1, largest - coarse, 0.0))
    parts = parts.astype(jnp.bfloat16)
    for group in range(groups):
        out_ref[group, :, :width] = (rotated_ref[group] * inverse).astype(out_ref.dtype)
        out_ref[group, :, width:] = parts


def transform(hidden, base, sign):
    groups, rows, width = hidden.shape
    low = base.shape[1]
    return pl.pallas_call(
        transform_kernel,
        out_shape=jax.ShapeDtypeStruct((groups, rows, width + LANES), jnp.bfloat16),
        in_specs=[pl.BlockSpec(memory_space=pltpu.VMEM)] * 3,
        out_specs=pl.BlockSpec(memory_space=pltpu.VMEM),
        scratch_shapes=[
            pltpu.VMEM((2, low, TILE), jnp.bfloat16),
            pltpu.VMEM((2, width // low, groups, rows, TILE), jnp.float32),
            pltpu.VMEM((groups, rows, width), jnp.float32),
        ],
        compiler_params=pltpu.CompilerParams(vmem_limit_bytes=VMEM_LIMIT),
        cost_estimate=pl.CostEstimate(
            flops=2 * groups * rows * width * low,
            bytes_accessed=4 * groups * rows * width,
            transcendentals=0,
        ),
        name="rotate_rows",
    )(hidden, base, sign)


def body(gate_pre, up_pre, rotation52):
    steps, rows, width = gate_pre.shape
    groups = lax.axis_size("tensor")
    base, sign = factor(rotation52)
    flat = (steps * rows, width)
    hidden = gated(gate_pre.reshape(flat), up_pre.reshape(flat))
    mine = lax.all_to_all(hidden.reshape(groups, -1, width), "tensor", 0, 0)
    packed = lax.all_to_all(transform(mine, base, sign), "tensor", 0, 0)
    return unpack(packed, steps, rows, width)


def solution(mesh):
    in_specs = (P(None, "dp", "tensor"), P(None, "dp", "tensor"), P())
    out_specs = (P(None, "dp", "tensor"), P(None, "dp"))
    return jax.shard_map(body, mesh=mesh, in_specs=in_specs, out_specs=out_specs, check_vma=False)
```

time: 115 us -> 111 us (0.965)
  waiting for transfers between devices: 33.6 us -> 40.2 us
  other arithmetic: 4.34 us -> 0 us
  local copies, waits for them, and re-layouts: 4.33 us -> 0.01 us
  Pallas kernels: 11.5 us -> 10.2 us
    all_to_all x1, waiting for transfers between devices: 33.6 us -> 40.2 us  [body(): mine = lax.all_to_all(hidden.reshape(groups, -1, width), 'tensor', 0, 0)]
    convert_element_type x1 -> x0, other arithmetic: 4.16 us -> none  [body(): (jax.nn.silu(gate_pre.astype(f32)) * up_pre.astype(f32)).astype(jnp.bfloa...]
    pallas_call x1, Pallas kernels: 6.48 us -> 4.09 us  [transform(): pl.pallas_call(transform_kernel, out_shape=jax.ShapeDtypeStruct((groups,...]
    unnamed x4 -> x2, local copies, waits for them, and re-layouts: 2.39 us -> 0.01 us
    slice x1 -> x0, local copies, waits for them, and re-layouts: 1.29 us -> none  [body(): quantized = packed[:, :, :width].reshape(steps, rows, width)]
    pallas_call x1 -> x3, Pallas kernels: 5.07 us -> 6.06 us  [the longest x1 3.42 us: gated(): pl.pallas_call(hidden_kernel, out_shape=jax.ShapeDtypeStruct(gate.shape,...]
  transfers between devices with their start and end apart: 1 -> 1, of which waited for: 1 -> 1; matrix products, arithmetic and copies ran while one was open for 0% -> 0% of each run, Pallas kernels for 4% -> 1%
where the time goes in v2:
time: 111 us
  blocking collectives  48.2 us (43%)
  waiting for transfers between devices  40.2 us (36%)
  starting transfers between devices  11.8 us (11%)
  Pallas kernels  10.2 us (9%)
    all_to_all x1, blocking collectives, body(): packed = lax.all_to_all(transform(mine, base, sign), 'tensor', 0, 0)  48.2 us
    all_to_all x1, waiting for transfers between devices, body(): mine = lax.all_to_all(hidden.reshape(groups, -1, width), 'tensor', 0, 0)  40.2 us
    all_to_all x1, starting transfers between devices, body(): mine = lax.all_to_all(hidden.reshape(groups, -1, width), 'tensor', 0, 0)  11.8 us
    pallas_call x1, Pallas kernels, transform(): pl.pallas_call(transform_kernel, out_shape=jax.ShapeDtypeStruct((groups,...  4.09 us
    pallas_call x1, Pallas kernels, gated(): pl.pallas_call(hidden_kernel, out_shape=jax.ShapeDtypeStruct(gate.shape,...  3.42 us
  transfers between devices with their start and end apart: 1, of which 1 were waited for; matrix products, arithmetic and copies ran while one was open for 0% of the time, Pallas kernels for 1%

profile of v2, /device:TPU:1, one launch (start us, length us, event | category | flops | bytes accessed | tf_op | source)
XLA Modules:
  0.0 111.1 jit_solution(4170172646869430616)
XLA Ops:
  0.6 3.4 %gated_hidden.1 = bf16[256,3328]{1,0:T(8,128)(2,1)} custom-call(bf16[256,3328]{1,0:T(8,128)(2,1)} %bitcast.5, bf16[256,3328]{1,0:T(8,128)(2,1)} %bitcast.6), custom_call_target="tpu_custom_call" | custom-call | flops 5111808 | bytes 5111808 | tf_op jit(solution)/shard_map/gated_hidden/pallas_call | solution.py:44
  4.1 0.0 copy-start
  4.1 11.8 %all-to-all-start = ((bf16[16,16,3328]{2,1,0:T(8,128)(2,1)}), bf16[16,16,3328]{2,1,0:T(8,128)(2,1)S(1)}, u32[]{:S(2)}, u32[]{:S(2)}) async-start(bf16[16,16,3328]{2,1,0:T(8,128)(2,1)} %bitcast.4), calls=%async_computation | async-start | bytes 3407872 | tf_op jit(solution)/shard_map/all_to_all | solution.py:261
  15.9 0.0 copy-done
  15.9 0.9 kron_factor.1
  16.8 40.2 %all-to-all-done.hidden_ref = bf16[16,16,3328]{2,1,0:T(8,128)(2,1)S(1)} async-done(((bf16[16,16,3328]{2,1,0:T(8,128)(2,1)}), bf16[16,16,3328]{2,1,0:T(8,128)(2,1)S(1)}, u32[]{:S(2)}, u32[]{:S(2)}) %all-to-all-start) | async-done | bytes 1703968 | tf_op jit(solution)/shard_map/all_to_all | solution.py:261
  57.0 4.1 %rotate_rows.1 = bf16[16,16,3456]{2,1,0:T(8,128)(2,1)S(1)} custom-call(bf16[16,16,3328]{2,1,0:T(8,128)(2,1)S(1)} %all-to-all-done.hidden_ref, bf16[208,1664]{1,0:T(8,128)(2,1)S(1)} %get-tuple-element.6.base_ref, bf16[16,1664]{1,0:T(8,128)(2,1)S(1)} %get-tuple-element.7.sign_ref), custom_call_target="tpu_custom_call" | custom-call | flops 2835349504 | bytes 3407872 | tf_op jit(solution)/shard_map/rotate_rows/pallas_call | solution.py:235
  61.1 48.2 %all_to_all.10.packed_ref = bf16[16,16,3456]{2,1,0:T(8,128)(2,1)S(1)} all-to-all(bf16[16,16,3456]{2,1,0:T(8,128)(2,1)S(1)} %rotate_rows.1), channel_id=1, replica_groups=mesh['dp'=32,'tensor'=16] {'tensor'}, dimensions={0} | all-to-all | bytes 3538944 | tf_op jit(solution)/shard_map/all_to_all | solution.py:262
  109.3 1.8 %unpack.1 = (bf16[16,16,3328]{2,1,0:T(8,128)(2,1)}, f32[2,128]{1,0:T(2,128)}) custom-call(bf16[16,16,3456]{2,1,0:T(8,128)(2,1)S(1)} %all_to_all.10.packed_ref), custom_call_target="tpu_custom_call" | custom-call | tf_op jit(solution)/shard_map/unpack/pallas_call | solution.py:85
Async XLA Ops:
  4.1 11.9 %copy-start = (bf16[52,52]{1,0:T(8,128)(2,1)S(1)}, bf16[52,52]{1,0:T(8,128)(2,1)}, u32[]{:S(2)}) copy-start(bf16[52,52]{1,0:T(8,128)(2,1)} %rotation_ref.1) | copy-start | bytes 16228
  4.1 52.9 %all-to-all-start = ((bf16[16,16,3328]{2,1,0:T(8,128)(2,1)}), bf16[16,16,3328]{2,1,0:T(8,128)(2,1)S(1)}, u32[]{:S(2)}, u32[]{:S(2)}) async-start(bf16[16,16,3328]{2,1,0:T(8,128)(2,1)} %bitcast.4), calls=%async_computation | async-start | bytes 3407872 | tf_op jit(solution)/shard_map/all_to_all | solution.py:261

commit v3 on v2

--- a/solution.py
+++ b/solution.py
@@ -13,9 +13,10 @@
 STREAM_LIMIT = 58 * 1024 * 1024
 
 
-def hidden_kernel(gate_hbm, up_hbm, out_ref, gate_ref, up_ref, sems):
+def hidden_kernel(gate_hbm, up_hbm, out_hbm, gate_ref, up_ref, out_ref, sems):
     chunks, rows, width = gate_ref.shape
     f32 = jnp.float32
+    block = 32
     copies = []
     for chunk in range(chunks):
         at = pl.ds(chunk * rows, rows)
@@ -23,18 +24,25 @@
             copy = pltpu.make_async_copy(source.at[at], target.at[chunk], sems.at[chunk, k])
             copy.start()
             copies.append(copy)
+    results = []
     for chunk in range(chunks):
         copies[2 * chunk].wait()
         copies[2 * chunk + 1].wait()
 
-        @pl.loop(0, rows // 16)
+        @pl.loop(0, rows // block)
         def _(step):
-            at = pl.ds(pl.multiple_of(step * 16, 16), 16)
+            at = pl.ds(pl.multiple_of(step * block, block), block)
             gate = gate_ref[chunk, at].astype(f32)
             half = 0.5 * gate
             silu = half * jnp.tanh(half) + half
-            value = (silu * up_ref[chunk, at].astype(f32)).astype(out_ref.dtype)
-            out_ref[pl.ds(pl.multiple_of(chunk * rows + step * 16, 16), 16), :] = value
+            out_ref[chunk, at] = (silu * up_ref[chunk, at].astype(f32)).astype(out_ref.dtype)
+
+        at = pl.ds(chunk * rows, rows)
+        result = pltpu.make_async_copy(out_ref.at[chunk], out_hbm.at[at], sems.at[chunk, 2])
+        result.start()
+        results.append(result)
+    for result in results:
+        result.wait()
 
 
 def gated(gate, up):
@@ -45,8 +53,8 @@
         hidden_kernel,
         out_shape=jax.ShapeDtypeStruct(gate.shape, gate.dtype),
         in_specs=[pl.BlockSpec(memory_space=pl.ANY)] * 2,
-        out_specs=pl.BlockSpec(memory_space=pltpu.VMEM),
-        scratch_shapes=[held, held, pltpu.SemaphoreType.DMA((chunks, 2))],
+        out_specs=pl.BlockSpec(memory_space=pl.ANY),
+        scratch_shapes=[held, held, held, pltpu.SemaphoreType.DMA((chunks, 3))],
         compiler_params=pltpu.CompilerParams(vmem_limit_bytes=STREAM_LIMIT),
         cost_estimate=pl.CostEstimate(
             flops=6 * rows * width, bytes_accessed=6 * rows * width, transcendentals=rows * width
@@ -203,10 +211,10 @@
                     group, half = divmod(i, halves)
                     column = half * low + starts[n] + lane
                     rotated_ref[group, at, column : column + LANES] = value
-                sizes = [jnp.abs(value) for value in values] + [peak[part]]
+                sizes = [jnp.abs(value) for value in values]
                 while len(sizes) > 1:
-                    sizes = [jnp.maximum(*sizes[:2])] + sizes[2:]
-                peak[part] = sizes[0]
+                    sizes = [jnp.maximum(*pair) for pair in zip(sizes[::2], sizes[1::2])]
+                peak[part] = jnp.maximum(peak[part], sizes[0])
 
     expand(0)
     for n in range(len(starts)):

time: 111 us -> 111 us (level)
  no operation moved by 1% of the time
where the time goes in v3:
time: 111 us
  blocking collectives  48.2 us (43%)
  waiting for transfers between devices  40.2 us (36%)
  starting transfers between devices  11.8 us (11%)
  Pallas kernels  9.75 us (9%)
    all_to_all x1, blocking collectives, body(): packed = lax.all_to_all(transform(mine, base, sign), 'tensor', 0, 0)  48.2 us
    all_to_all x1, waiting for transfers between devices, body(): mine = lax.all_to_all(hidden.reshape(groups, -1, width), 'tensor', 0, 0)  40.2 us
    all_to_all x1, starting transfers between devices, body(): mine = lax.all_to_all(hidden.reshape(groups, -1, width), 'tensor', 0, 0)  11.8 us
    pallas_call x1, Pallas kernels, transform(): pl.pallas_call(transform_kernel, out_shape=jax.ShapeDtypeStruct((groups,...  4.09 us
    pallas_call x1, Pallas kernels, gated(): pl.pallas_call(hidden_kernel, out_shape=jax.ShapeDtypeStruct(gate.shape,...  3.01 us
  transfers between devices with their start and end apart: 1, of which 1 were waited for; matrix products, arithmetic and copies ran while one was open for 0% of the time, Pallas kernels for 1%

profile of v3, /device:TPU:1, one launch (start us, length us, event | category | flops | bytes accessed | tf_op | source)
XLA Modules:
  0.0 110.7 jit_solution(16765788320847637398)
XLA Ops:
  0.6 3.0 %gated_hidden.1 = bf16[256,3328]{1,0:T(8,128)(2,1)} custom-call(bf16[256,3328]{1,0:T(8,128)(2,1)} %bitcast.5, bf16[256,3328]{1,0:T(8,128)(2,1)} %bitcast.6), custom_call_target="tpu_custom_call" | custom-call | flops 5111808 | bytes 5111808 | tf_op jit(solution)/shard_map/gated_hidden/pallas_call | solution.py:52
  3.6 0.0 copy-start
  3.7 11.8 %all-to-all-start = ((bf16[16,16,3328]{2,1,0:T(8,128)(2,1)}), bf16[16,16,3328]{2,1,0:T(8,128)(2,1)S(1)}, u32[]{:S(2)}, u32[]{:S(2)}) async-start(bf16[16,16,3328]{2,1,0:T(8,128)(2,1)} %bitcast.4), calls=%async_computation | async-start | bytes 3407872 | tf_op jit(solution)/shard_map/all_to_all | solution.py:269
  15.5 0.0 copy-done
  15.5 0.9 kron_factor.1
  16.4 40.2 %all-to-all-done.hidden_ref = bf16[16,16,3328]{2,1,0:T(8,128)(2,1)S(1)} async-done(((bf16[16,16,3328]{2,1,0:T(8,128)(2,1)}), bf16[16,16,3328]{2,1,0:T(8,128)(2,1)S(1)}, u32[]{:S(2)}, u32[]{:S(2)}) %all-to-all-start) | async-done | bytes 1703968 | tf_op jit(solution)/shard_map/all_to_all | solution.py:269
  56.6 4.1 %rotate_rows.1 = bf16[16,16,3456]{2,1,0:T(8,128)(2,1)S(1)} custom-call(bf16[16,16,3328]{2,1,0:T(8,128)(2,1)S(1)} %all-to-all-done.hidden_ref, bf16[208,1664]{1,0:T(8,128)(2,1)S(1)} %get-tuple-element.6.base_ref, bf16[16,1664]{1,0:T(8,128)(2,1)S(1)} %get-tuple-element.7.sign_ref), custom_call_target="tpu_custom_call" | custom-call | flops 2835349504 | bytes 3407872 | tf_op jit(solution)/shard_map/rotate_rows/pallas_call | solution.py:243
  60.7 48.2 %all_to_all.10.packed_ref = bf16[16,16,3456]{2,1,0:T(8,128)(2,1)S(1)} all-to-all(bf16[16,16,3456]{2,1,0:T(8,128)(2,1)S(1)} %rotate_rows.1), channel_id=1, replica_groups=mesh['dp'=32,'tensor'=16] {'tensor'}, dimensions={0} | all-to-all | bytes 3538944 | tf_op jit(solution)/shard_map/all_to_all | solution.py:270
  108.9 1.8 %unpack.1 = (bf16[16,16,3328]{2,1,0:T(8,128)(2,1)}, f32[2,128]{1,0:T(2,128)}) custom-call(bf16[16,16,3456]{2,1,0:T(8,128)(2,1)S(1)} %all_to_all.10.packed_ref), custom_call_target="tpu_custom_call" | custom-call | tf_op jit(solution)/shard_map/unpack/pallas_call | solution.py:93
Async XLA Ops:
  3.6 11.9 %copy-start = (bf16[52,52]{1,0:T(8,128)(2,1)S(1)}, bf16[52,52]{1,0:T(8,128)(2,1)}, u32[]{:S(2)}) copy-start(bf16[52,52]{1,0:T(8,128)(2,1)} %rotation_ref.1) | copy-start | bytes 16228
  3.7 52.9 %all-to-all-start = ((bf16[16,16,3328]{2,1,0:T(8,128)(2,1)}), bf16[16,16,3328]{2,1,0:T(8,128)(2,1)S(1)}, u32[]{:S(2)}, u32[]{:S(2)}) async-start(bf16[16,16,3328]{2,1,0:T(8,128)(2,1)} %bitcast.4), calls=%async_computation | async-start | bytes 3407872 | tf_op jit(solution)/shard_map/all_to_all | solution.py:269

commit v4 on v3

--- a/solution.py
+++ b/solution.py
@@ -6,9 +6,10 @@
 from jax.sharding import PartitionSpec as P
 
 HAD_BIG = 1024
-LOW = 32
 LANES = 128
-TILE = 2 * LANES
+LOW = 8
+PARTS = 4
+WINDOW = 512
 VMEM_LIMIT = 20 * 1024 * 1024
 STREAM_LIMIT = 58 * 1024 * 1024
 
@@ -108,14 +109,16 @@
 def parity_sign(left, right):
     both = left & right
     parity = both
-    for level in (1, 2, 3, 4):
+    for level in (1, 2):
         parity = parity ^ (both >> level)
     return 1 - 2 * (parity & 1)
 
 
-def factor_kernel(rotation_ref, base_ref, sign_ref):
+def factor_kernel(rotation_ref, out_ref):
     small = rotation_ref.shape[0]
-    height, width = base_ref.shape
+    size = LOW * small
+    height, width = out_ref.shape
+    margin = height - width
     f32, bf16 = jnp.float32, jnp.bfloat16
 
     def block(index):
@@ -127,33 +130,33 @@
     def one_where(mask):
         return mask.astype(f32).astype(bf16)
 
-    lane = iota((small, width), 1)
-    across = one_where(lane - block(lane) * small == iota((small, width), 0))
+    shape = (small, width)
+    lane = iota(shape, 1)
+    across = one_where((lane - block(lane) * small == iota(shape, 0)) & (lane < size))
     tiled = jnp.dot(rotation_ref[...], across, preferred_element_type=f32).astype(bf16)
-    row = iota((height, small), 0)
-    down = one_where(row - block(row) * small == iota((height, small), 1))
+    shape = (height, small)
+    row = iota(shape, 0) - margin
+    inside = (row >= 0) & (row < size)
+    down = one_where((row - block(row) * small == iota(shape, 1)) & inside)
     value = jnp.dot(down, tiled, preferred_element_type=f32)
     shape = (height, width)
-    sign = parity_sign(block(iota(shape, 0)), block(iota(shape, 1))).astype(f32)
-    base_ref[...] = (value * sign).astype(bf16)
-    shape = sign_ref.shape
-    sign_ref[...] = parity_sign(4 * iota(shape, 0), block(iota(shape, 1))).astype(f32).astype(bf16)
+    sign = parity_sign(block(iota(shape, 0) - margin), block(iota(shape, 1))).astype(f32)
+    out_ref[...] = (value * sign).astype(bf16)
 
 
 def factor(rotation52):
     small = rotation52.shape[0]
-    width = LOW * small
+    margin = WINDOW - LOW * small
     return pl.pallas_call(
         factor_kernel,
-        out_shape=(
-            jax.ShapeDtypeStruct((4 * small, width), jnp.bfloat16),
-            jax.ShapeDtypeStruct((16, width), jnp.bfloat16),
-        ),
+        out_shape=jax.ShapeDtypeStruct((margin + WINDOW, WINDOW), jnp.bfloat16),
         in_specs=[pl.BlockSpec(memory_space=pltpu.VMEM)],
-        out_specs=[pl.BlockSpec(memory_space=pltpu.VMEM)] * 2,
+        out_specs=pl.BlockSpec(memory_space=pltpu.VMEM),
         compiler_params=pltpu.CompilerParams(vmem_limit_bytes=VMEM_LIMIT),
         cost_estimate=pl.CostEstimate(
-            flops=2 * 4 * small * width * 52, bytes_accessed=8 * small * width, transcendentals=0
+            flops=2 * (margin + WINDOW) * WINDOW * small,
+            bytes_accessed=2 * (margin + WINDOW) * WINDOW,
+            transcendentals=0,
         ),
         name="kron_factor",
     )(rotation52)
@@ -171,59 +174,83 @@
     return values
 
 
-def transform_kernel(hidden_ref, base_ref, sign_ref, out_ref, factor_ref, product_ref, rotated_ref):
+def transform_kernel(hidden_ref, factor_ref, out_ref, product_ref, middle_ref, rotated_ref):
     groups, rows, width = hidden_ref.shape
-    height, low = base_ref.shape
-    halves = width // low
+    margin = factor_ref.shape[0] - WINDOW
+    size = WINDOW - margin
+    span = PARTS * size
+    halves = width // span
     f32 = jnp.float32
-    starts = list(range(0, low, TILE))
-    peak = [jnp.zeros((8, LANES), f32) for _ in range(rows // 8)]
-
-    def expand(n):
-        size = min(TILE, low - starts[n])
-        at = slice(starts[n], starts[n] + size)
-        for i in range(low // height):
-            factor_ref[n % 2, i * height : (i + 1) * height, :size] = (
-                base_ref[:, at] * sign_ref[i : i + 1, at]
-            )
-
-    def multiply(n):
-        size = min(TILE, low - starts[n])
+    tiles = WINDOW // LANES
+    row_tiles = [slice(at, at + 8) for at in range(0, rows, 8)]
+    peak = [jnp.zeros((8, LANES), f32) for _ in row_tiles]
+    lane = lax.broadcasted_iota(jnp.int32, (8, LANES), 1)
+
+    def multiply(part):
+        window = part * size // LANES * LANES
+        start = margin - (part * size - window)
         for half in range(halves):
-            product_ref[n % 2, half, :, :, :size] = jnp.dot(
-                hidden_ref[:, :, half * low : (half + 1) * low].reshape(groups * rows, low),
-                factor_ref[n % 2, :, :size],
+            at = half * span + window
+            product_ref[part % 2, half] = jnp.dot(
+                hidden_ref[:, :, at : at + WINDOW].reshape(groups * rows, WINDOW),
+                factor_ref[start : start + WINDOW, :],
                 preferred_element_type=f32,
-            ).reshape(groups, rows, size)
-
-    def combine(n):
-        for part in range(rows // 8):
-            at = slice(part * 8, part * 8 + 8)
-            for lane in range(0, min(TILE, low - starts[n]), LANES):
+            ).reshape(groups, rows, WINDOW)
+
+    def combine(part):
+        for at in row_tiles:
+            for tile in range(tiles):
+                column = slice(tile * LANES, (tile + 1) * LANES)
                 values = butterfly(
                     [
-                        product_ref[n % 2, half, group, at, lane : lane + LANES]
+                        product_ref[part % 2, half, group, at, column]
                         for group in range(groups)
                         for half in range(halves)
                     ]
                 )
                 for i, value in enumerate(values):
                     group, half = divmod(i, halves)
-                    column = half * low + starts[n] + lane
-                    rotated_ref[group, at, column : column + LANES] = value
-                sizes = [jnp.abs(value) for value in values]
-                while len(sizes) > 1:
-                    sizes = [jnp.maximum(*pair) for pair in zip(sizes[::2], sizes[1::2])]
-                peak[part] = jnp.maximum(peak[part], sizes[0])
-
-    expand(0)
-    for n in range(len(starts)):
-        if n + 1 < len(starts):
-            expand(n + 1)
-        multiply(n)
-        if n > 0:
-            combine(n - 1)
-    combine(len(starts) - 1)
+                    middle_ref[part, half, group, at, column] = value
+
+    def place(group, half, k):
+        at = row_tiles[k]
+        parts = [[] for _ in range(PARTS)]
+        for tile in range(tiles):
+            column = slice(tile * LANES, (tile + 1) * LANES)
+            values = butterfly([middle_ref[part, half, group, at, column] for part in range(PARTS)])
+            for part, value in enumerate(values):
+                shift = part * size % LANES
+                parts[part].append(pltpu.roll(value, shift, 1) if shift else value)
+        placed = []
+        for part in range(PARTS):
+            shift = part * size % LANES
+            values = parts[part]
+            if part > 0:
+                placed[-1] = jnp.where(lane < shift, placed[-1], values[0])
+                values = values[:1] + [
+                    jnp.where(lane < shift, values[tile - 1], values[tile]) for tile in range(1, tiles)
+                ]
+                placed += values[1:]
+            else:
+                placed += values
+        for i, value in enumerate(placed):
+            column = half * span + i * LANES
+            rotated_ref[group, at, column : column + LANES] = value
+        sizes = [jnp.abs(value) for value in placed] + [peak[k]]
+        while len(sizes) > 1:
+            pairs = [jnp.maximum(*sizes[i : i + 2]) for i in range(0, len(sizes) - 1, 2)]
+            sizes = pairs + sizes[2 * len(pairs) :]
+        peak[k] = sizes[0]
+
+    multiply(0)
+    for part in range(PARTS):
+        if part + 1 < PARTS:
+            multiply(part + 1)
+        combine(part)
+    for group in range(groups):
+        for half in range(halves):
+            for k in range(len(row_tiles)):
+                place(group, half, k)
     scale = HAD_BIG**-0.5
     largest = jnp.concatenate([jnp.max(p, axis=1, keepdims=True) for p in peak], axis=0)
     largest = largest * scale + 1e-6
@@ -237,37 +264,37 @@
         out_ref[group, :, width:] = parts
 
 
-def transform(hidden, base, sign):
+def transform(hidden, weights):
     groups, rows, width = hidden.shape
-    low = base.shape[1]
+    halves = width // (PARTS * (2 * WINDOW - weights.shape[0]))
     return pl.pallas_call(
         transform_kernel,
         out_shape=jax.ShapeDtypeStruct((groups, rows, width + LANES), jnp.bfloat16),
-        in_specs=[pl.BlockSpec(memory_space=pltpu.VMEM)] * 3,
+        in_specs=[pl.BlockSpec(memory_space=pltpu.VMEM)] * 2,
         out_specs=pl.BlockSpec(memory_space=pltpu.VMEM),
         scratch_shapes=[
-            pltpu.VMEM((2, low, TILE), jnp.bfloat16),
-            pltpu.VMEM((2, width // low, groups, rows, TILE), jnp.float32),
+            pltpu.VMEM((2, halves, groups, rows, WINDOW), jnp.float32),
+            pltpu.VMEM((PARTS, halves, groups, rows, WINDOW), jnp.float32),
             pltpu.VMEM((groups, rows, width), jnp.float32),
         ],
         compiler_params=pltpu.CompilerParams(vmem_limit_bytes=VMEM_LIMIT),
         cost_estimate=pl.CostEstimate(
-            flops=2 * groups * rows * width * low,
+            flops=2 * groups * rows * PARTS * halves * WINDOW * WINDOW,
             bytes_accessed=4 * groups * rows * width,
             transcendentals=0,
         ),
         name="rotate_rows",
-    )(hidden, base, sign)
+    )(hidden, weights)
 
 
 def body(gate_pre, up_pre, rotation52):
     steps, rows, width = gate_pre.shape
     groups = lax.axis_size("tensor")
-    base, sign = factor(rotation52)
+    weights = factor(rotation52)
     flat = (steps * rows, width)
     hidden = gated(gate_pre.reshape(flat), up_pre.reshape(flat))
     mine = lax.all_to_all(hidden.reshape(groups, -1, width), "tensor", 0, 0)
-    packed = lax.all_to_all(transform(mine, base, sign), "tensor", 0, 0)
+    packed = lax.all_to_all(transform(mine, weights), "tensor", 0, 0)
     return unpack(packed, steps, rows, width)
 
 

time: 111 us -> 110 us (level)
  Pallas kernels: 9.75 us -> 8.51 us
where the time goes in v4:
time: 110 us
  blocking collectives  48.2 us (44%)
  waiting for transfers between devices  40.4 us (37%)
  starting transfers between devices  11.8 us (11%)
  Pallas kernels  8.51 us (8%)
    all_to_all x1, blocking collectives, body(): packed = lax.all_to_all(transform(mine, weights), 'tensor', 0, 0)  48.2 us
    all_to_all x1, waiting for transfers between devices, body(): mine = lax.all_to_all(hidden.reshape(groups, -1, width), 'tensor', 0, 0)  40.4 us
    all_to_all x1, starting transfers between devices, body(): mine = lax.all_to_all(hidden.reshape(groups, -1, width), 'tensor', 0, 0)  11.8 us
    pallas_call x1, Pallas kernels, transform(): pl.pallas_call(transform_kernel, out_shape=jax.ShapeDtypeStruct((groups,...  3.05 us
    pallas_call x1, Pallas kernels, gated(): pl.pallas_call(hidden_kernel, out_shape=jax.ShapeDtypeStruct(gate.shape,...  3.01 us
  transfers between devices with their start and end apart: 1, of which 1 were waited for; matrix products, arithmetic and copies ran while one was open for 0% of the time, Pallas kernels for 1%

profile of v4, /device:TPU:1, one launch (start us, length us, event | category | flops | bytes accessed | tf_op | source)
XLA Modules:
  0.0 109.6 jit_solution(2381581547761887095)
XLA Ops:
  0.6 3.0 %gated_hidden.1 = bf16[256,3328]{1,0:T(8,128)(2,1)} custom-call(bf16[256,3328]{1,0:T(8,128)(2,1)} %bitcast.5, bf16[256,3328]{1,0:T(8,128)(2,1)} %bitcast.6), custom_call_target="tpu_custom_call" | custom-call | flops 5111808 | bytes 5111808 | tf_op jit(solution)/shard_map/gated_hidden/pallas_call | solution.py:53
  3.6 0.0 copy-start
  3.7 11.8 %all-to-all-start = ((bf16[16,16,3328]{2,1,0:T(8,128)(2,1)}), bf16[16,16,3328]{2,1,0:T(8,128)(2,1)S(1)}, u32[]{:S(2)}, u32[]{:S(2)}) async-start(bf16[16,16,3328]{2,1,0:T(8,128)(2,1)} %bitcast.4), calls=%async_computation | async-start | bytes 3407872 | tf_op jit(solution)/shard_map/all_to_all | solution.py:296
  15.5 0.0 copy-done
  15.5 0.7 kron_factor.1.factor_ref
  16.2 40.4 %all-to-all-done.hidden_ref = bf16[16,16,3328]{2,1,0:T(8,128)(2,1)S(1)} async-done(((bf16[16,16,3328]{2,1,0:T(8,128)(2,1)}), bf16[16,16,3328]{2,1,0:T(8,128)(2,1)S(1)}, u32[]{:S(2)}, u32[]{:S(2)}) %all-to-all-start) | async-done | bytes 1703968 | tf_op jit(solution)/shard_map/all_to_all | solution.py:296
  56.6 3.1 %rotate_rows.1 = bf16[16,16,3456]{2,1,0:T(8,128)(2,1)S(1)} custom-call(bf16[16,16,3328]{2,1,0:T(8,128)(2,1)S(1)} %all-to-all-done.hidden_ref, bf16[608,512]{1,0:T(8,128)(2,1)S(1)} %kron_factor.1.factor_ref), custom_call_target="tpu_custom_call" | custom-call | flops 1073741824 | bytes 3407872 | tf_op jit(solution)/shard_map/rotate_rows/pallas_call | solution.py:270
  59.6 48.2 %all_to_all.10.packed_ref = bf16[16,16,3456]{2,1,0:T(8,128)(2,1)S(1)} all-to-all(bf16[16,16,3456]{2,1,0:T(8,128)(2,1)S(1)} %rotate_rows.1), channel_id=1, replica_groups=mesh['dp'=32,'tensor'=16] {'tensor'}, dimensions={0} | all-to-all | bytes 3538944 | tf_op jit(solution)/shard_map/all_to_all | solution.py:297
  107.9 1.8 %unpack.1 = (bf16[16,16,3328]{2,1,0:T(8,128)(2,1)}, f32[2,128]{1,0:T(2,128)}) custom-call(bf16[16,16,3456]{2,1,0:T(8,128)(2,1)S(1)} %all_to_all.10.packed_ref), custom_call_target="tpu_custom_call" | custom-call | tf_op jit(solution)/shard_map/unpack/pallas_call | solution.py:94
Async XLA Ops:
  3.6 11.9 %copy-start = (bf16[52,52]{1,0:T(8,128)(2,1)S(1)}, bf16[52,52]{1,0:T(8,128)(2,1)}, u32[]{:S(2)}) copy-start(bf16[52,52]{1,0:T(8,128)(2,1)} %rotation_ref.1) | copy-start | bytes 16228
  3.7 52.9 %all-to-all-start = ((bf16[16,16,3328]{2,1,0:T(8,128)(2,1)}), bf16[16,16,3328]{2,1,0:T(8,128)(2,1)S(1)}, u32[]{:S(2)}, u32[]{:S(2)}) async-start(bf16[16,16,3328]{2,1,0:T(8,128)(2,1)} %bitcast.4), calls=%async_computation | async-start | bytes 3407872 | tf_op jit(solution)/shard_map/all_to_all | solution.py:296

commit v5 on v4

--- a/solution.py
+++ b/solution.py
@@ -10,6 +10,7 @@
 LOW = 8
 PARTS = 4
 WINDOW = 512
+SIDE = WINDOW // 2
 VMEM_LIMIT = 20 * 1024 * 1024
 STREAM_LIMIT = 58 * 1024 * 1024
 
@@ -64,42 +65,57 @@
     )(gate, up)
 
 
-def unpack_kernel(packed_ref, out_hbm, peak_ref, sem):
-    groups, rows, packed = packed_ref.shape
-    width = out_hbm.shape[2]
+def unpack_kernel(packed_ref, out_hbm, peak_ref, held_ref, sems):
+    groups, rows, width = held_ref.shape
     steps, span = peak_ref.shape
-    per = groups // steps
+    count = sems.shape[0]
+    each = groups // count
+    f32, bf16 = jnp.float32, jnp.bfloat16
     copies = []
-    count = sem.shape[0]
     for part in range(count):
-        at = pl.ds(part * (groups // count), groups // count)
-        copy = pltpu.make_async_copy(
-            packed_ref.at[at, :, pl.ds(0, width)], out_hbm.at[at], sem.at[part]
-        )
+        for group in range(part * each, part * each + each):
+            for i in range(width // LANES):
+                value = packed_ref[group, i * rows : (i + 1) * rows, :]
+                held_ref[group, :, i * LANES : (i + 1) * LANES] = value
+        at = pl.ds(part * each, each)
+        copy = pltpu.make_async_copy(held_ref.at[at], out_hbm.at[at], sems.at[part])
         copy.start()
         copies.append(copy)
-    lanes = lax.broadcasted_iota(jnp.int32, (8, packed - width), 1)
-    both = (lanes < 2).astype(jnp.float32).astype(jnp.bfloat16)
+
+    def iota(shape, dim):
+        return lax.broadcasted_iota(jnp.int32, shape, dim)
+
+    parts = packed_ref[:, width // LANES * rows :, :].astype(f32).reshape(groups * 8, LANES)
+    pick = (iota((8, LANES), 0) == iota((8, LANES), 1)).astype(f32).astype(bf16)
+    turned = lax.dot_general(
+        pick, parts.astype(bf16), (((1,), (1,)), ((), ())), preferred_element_type=f32
+    ).astype(bf16)
+    shape = (groups * 8, groups * rows)
+    source, target = iota(shape, 0), iota(shape, 1)
+    peaks = jnp.zeros((1, groups * rows), f32)
+    for k in range(rows // 8):
+        place = (target == (source >> 3) * rows + k * 8 + (source & 7)).astype(f32).astype(bf16)
+        moved = jnp.dot(turned, place, preferred_element_type=f32)
+        peaks = peaks + (moved[2 * k : 2 * k + 1] + moved[2 * k + 1 : 2 * k + 2])
     for step in range(steps):
-        parts = packed_ref[step * per : step * per + per, :, width:].reshape(span, packed - width)
-        sums = lax.dot_general(
-            both, parts, (((1,), (1,)), ((), ())), preferred_element_type=jnp.float32
-        )
-        peak_ref[step : step + 1, :] = sums[:1]
+        peak_ref[step : step + 1, :] = peaks[:, step * span : (step + 1) * span]
     for copy in copies:
         copy.wait()
 
 
 def unpack(packed, steps, span, width):
+    groups = packed.shape[0]
+    rows = steps * span // groups
+    shape = (groups, rows, width)
     quantized, peaks = pl.pallas_call(
         unpack_kernel,
         out_shape=(
-            jax.ShapeDtypeStruct((*packed.shape[:2], width), packed.dtype),
+            jax.ShapeDtypeStruct(shape, packed.dtype),
             jax.ShapeDtypeStruct((steps, span), jnp.float32),
         ),
         in_specs=[pl.BlockSpec(memory_space=pltpu.VMEM)],
         out_specs=(pl.BlockSpec(memory_space=pl.ANY), pl.BlockSpec(memory_space=pltpu.VMEM)),
-        scratch_shapes=[pltpu.SemaphoreType.DMA((4,))],
+        scratch_shapes=[pltpu.VMEM(shape, packed.dtype), pltpu.SemaphoreType.DMA((4,))],
         compiler_params=pltpu.CompilerParams(vmem_limit_bytes=VMEM_LIMIT),
         name="unpack",
     )(packed)
@@ -181,25 +197,24 @@
     span = PARTS * size
     halves = width // span
     f32 = jnp.float32
-    tiles = WINDOW // LANES
     row_tiles = [slice(at, at + 8) for at in range(0, rows, 8)]
     peak = [jnp.zeros((8, LANES), f32) for _ in row_tiles]
     lane = lax.broadcasted_iota(jnp.int32, (8, LANES), 1)
 
-    def multiply(part):
+    def multiply(part, side):
         window = part * size // LANES * LANES
         start = margin - (part * size - window)
         for half in range(halves):
             at = half * span + window
             product_ref[part % 2, half] = jnp.dot(
                 hidden_ref[:, :, at : at + WINDOW].reshape(groups * rows, WINDOW),
-                factor_ref[start : start + WINDOW, :],
+                factor_ref[start : start + WINDOW, side * SIDE : (side + 1) * SIDE],
                 preferred_element_type=f32,
-            ).reshape(groups, rows, WINDOW)
-
-    def combine(part):
+            ).reshape(groups, rows, SIDE)
+
+    def combine(part, side):
         for at in row_tiles:
-            for tile in range(tiles):
+            for tile in range(SIDE // LANES):
                 column = slice(tile * LANES, (tile + 1) * LANES)
                 values = butterfly(
                     [
@@ -208,60 +223,85 @@
                         for half in range(halves)
                     ]
                 )
+                column = slice(side * SIDE + tile * LANES, side * SIDE + (tile + 1) * LANES)
                 for i, value in enumerate(values):
                     group, half = divmod(i, halves)
                     middle_ref[part, half, group, at, column] = value
 
-    def place(group, half, k):
+    def place(group, half, k, side):
         at = row_tiles[k]
-        parts = [[] for _ in range(PARTS)]
-        for tile in range(tiles):
+        shifts = [part * size % LANES for part in range(PARTS)]
+        moved = [[] for _ in range(PARTS)]
+        for tile in range(2 * side, 2 * side + 2):
             column = slice(tile * LANES, (tile + 1) * LANES)
             values = butterfly([middle_ref[part, half, group, at, column] for part in range(PARTS)])
             for part, value in enumerate(values):
-                shift = part * size % LANES
-                parts[part].append(pltpu.roll(value, shift, 1) if shift else value)
-        placed = []
-        for part in range(PARTS):
-            shift = part * size % LANES
-            values = parts[part]
-            if part > 0:
-                placed[-1] = jnp.where(lane < shift, placed[-1], values[0])
-                values = values[:1] + [
-                    jnp.where(lane < shift, values[tile - 1], values[tile]) for tile in range(1, tiles)
-                ]
-                placed += values[1:]
+                moved[part].append(pltpu.roll(value, shifts[part], 1) if part else value)
+
+        def tile_at(i):
+            column = half * span + i * LANES
+            return group, at, slice(column, column + LANES)
+
+        whole = {}
+        for part, (left, right) in enumerate(moved):
+            first = part * size // LANES
+            if side == 0:
+                if part == 0:
+                    whole[first] = left
+                    whole[first + 1] = right
+                else:
+                    rotated_ref[tile_at(first)] = left
+                    whole[first + 1] = jnp.where(lane < shifts[part], left, right)
+                    rotated_ref[tile_at(first + 2)] = right
             else:
-                placed += values
-        for i, value in enumerate(placed):
-            column = half * span + i * LANES
-            rotated_ref[group, at, column : column + LANES] = value
-        sizes = [jnp.abs(value) for value in placed] + [peak[k]]
+                if part > 0:
+                    waiting = rotated_ref[tile_at(first + 2)]
+                    right = jnp.where(lane < shifts[part], left, right)
+                    left = jnp.where(lane < shifts[part], waiting, left)
+                if part + 1 < PARTS:
+                    right = jnp.where(lane < shifts[part + 1], right, rotated_ref[tile_at(first + 3)])
+                whole[first + 2] = left
+                whole[first + 3] = right
+        for i, value in whole.items():
+            rotated_ref[tile_at(i)] = value
+        sizes = [jnp.abs(value) for value in whole.values()]
         while len(sizes) > 1:
             pairs = [jnp.maximum(*sizes[i : i + 2]) for i in range(0, len(sizes) - 1, 2)]
             sizes = pairs + sizes[2 * len(pairs) :]
-        peak[k] = sizes[0]
-
-    multiply(0)
-    for part in range(PARTS):
-        if part + 1 < PARTS:
-            multiply(part + 1)
-        combine(part)
-    for group in range(groups):
-        for half in range(halves):
-            for k in range(len(row_tiles)):
-                place(group, half, k)
+        peak[k] = jnp.maximum(peak[k], sizes[0])
+
+    units = [
+        (group, half, k)
+        for k in range(len(row_tiles))
+        for half in range(halves)
+        for group in range(groups)
+    ]
+    steps = [(part, side) for side in range(2) for part in range(PARTS)]
+    multiply(*steps[0])
+    for i, (part, side) in enumerate(steps):
+        if i + 1 < len(steps):
+            multiply(*steps[i + 1])
+        combine(part, side)
+        if side > 0:
+            for unit in units[part::PARTS]:
+                place(*unit, 0)
+    for unit in units:
+        place(*unit, 1)
     scale = HAD_BIG**-0.5
     largest = jnp.concatenate([jnp.max(p, axis=1, keepdims=True) for p in peak], axis=0)
     largest = largest * scale + 1e-6
     inverse = scale / largest
     coarse = largest.astype(jnp.bfloat16).astype(f32)
-    lanes = lax.broadcasted_iota(jnp.int32, (rows, LANES), 1)
-    parts = jnp.where(lanes == 0, coarse, jnp.where(lanes == 1, largest - coarse, 0.0))
+    parts = jnp.zeros((8, LANES), f32)
+    for k, at in enumerate(row_tiles):
+        parts = jnp.where(lane == 2 * k, coarse[at], parts)
+        parts = jnp.where(lane == 2 * k + 1, (largest - coarse)[at], parts)
     parts = parts.astype(jnp.bfloat16)
     for group in range(groups):
-        out_ref[group, :, :width] = (rotated_ref[group] * inverse).astype(out_ref.dtype)
-        out_ref[group, :, width:] = parts
+        for i in range(width // LANES):
+            value = rotated_ref[group, :, i * LANES : (i + 1) * LANES] * inverse
+            out_ref[group, i * rows : (i + 1) * rows, :] = value.astype(out_ref.dtype)
+        out_ref[group, width // LANES * rows :, :] = parts
 
 
 def transform(hidden, weights):
@@ -269,11 +309,11 @@
     halves = width // (PARTS * (2 * WINDOW - weights.shape[0]))
     return pl.pallas_call(
         transform_kernel,
-        out_shape=jax.ShapeDtypeStruct((groups, rows, width + LANES), jnp.bfloat16),
+        out_shape=jax.ShapeDtypeStruct((groups, width // LANES * rows + 8, LANES), jnp.bfloat16),
         in_specs=[pl.BlockSpec(memory_space=pltpu.VMEM)] * 2,
         out_specs=pl.BlockSpec(memory_space=pltpu.VMEM),
         scratch_shapes=[
-            pltpu.VMEM((2, halves, groups, rows, WINDOW), jnp.float32),
+            pltpu.VMEM((2, halves, groups, rows, SIDE), jnp.float32),
             pltpu.VMEM((PARTS, halves, groups, rows, WINDOW), jnp.float32),
             pltpu.VMEM((groups, rows, width), jnp.float32),
         ],

time: 110 us -> 109 us (level)
  no operation moved by 1% of the time
where the time goes in v5:
time: 109 us
  blocking collectives  47.6 us (44%)
  waiting for transfers between devices  40.4 us (37%)
  starting transfers between devices  11.8 us (11%)
  Pallas kernels  8.18 us (8%)
    all_to_all x1, blocking collectives, body(): packed = lax.all_to_all(transform(mine, weights), 'tensor', 0, 0)  47.6 us
    all_to_all x1, waiting for transfers between devices, body(): mine = lax.all_to_all(hidden.reshape(groups, -1, width), 'tensor', 0, 0)  40.4 us
    all_to_all x1, starting transfers between devices, body(): mine = lax.all_to_all(hidden.reshape(groups, -1, width), 'tensor', 0, 0)  11.8 us
    pallas_call x1, Pallas kernels, gated(): pl.pallas_call(hidden_kernel, out_shape=jax.ShapeDtypeStruct(gate.shape,...  3.01 us
    pallas_call x1, Pallas kernels, transform(): pl.pallas_call(transform_kernel, out_shape=jax.ShapeDtypeStruct((groups,...  2.56 us
  transfers between devices with their start and end apart: 1, of which 1 were waited for; matrix products, arithmetic and copies ran while one was open for 0% of the time, Pallas kernels for 1%

profile of v5, /device:TPU:1, one launch (start us, length us, event | category | flops | bytes accessed | tf_op | source)
XLA Modules:
  0.0 108.6 jit_solution(15566582296914027596)
XLA Ops:
  0.6 3.0 %gated_hidden.1 = bf16[256,3328]{1,0:T(8,128)(2,1)} custom-call(bf16[256,3328]{1,0:T(8,128)(2,1)} %bitcast.5, bf16[256,3328]{1,0:T(8,128)(2,1)} %bitcast.6), custom_call_target="tpu_custom_call" | custom-call | flops 5111808 | bytes 5111808 | tf_op jit(solution)/shard_map/gated_hidden/pallas_call | solution.py:54
  3.6 0.0 copy-start
  3.7 11.8 %all-to-all-start = ((bf16[16,16,3328]{2,1,0:T(8,128)(2,1)}), bf16[16,16,3328]{2,1,0:T(8,128)(2,1)S(1)}, u32[]{:S(2)}, u32[]{:S(2)}) async-start(bf16[16,16,3328]{2,1,0:T(8,128)(2,1)} %bitcast.4), calls=%async_computation | async-start | bytes 3407872 | tf_op jit(solution)/shard_map/all_to_all | solution.py:336
  15.5 0.0 copy-done
  15.5 0.7 kron_factor.1.factor_ref
  16.2 40.4 %all-to-all-done.hidden_ref = bf16[16,16,3328]{2,1,0:T(8,128)(2,1)S(1)} async-done(((bf16[16,16,3328]{2,1,0:T(8,128)(2,1)}), bf16[16,16,3328]{2,1,0:T(8,128)(2,1)S(1)}, u32[]{:S(2)}, u32[]{:S(2)}) %all-to-all-start) | async-done | bytes 1703968 | tf_op jit(solution)/shard_map/all_to_all | solution.py:336
  56.6 2.6 %rotate_rows.1 = bf16[16,424,128]{2,1,0:T(8,128)(2,1)S(1)} custom-call(bf16[16,16,3328]{2,1,0:T(8,128)(2,1)S(1)} %all-to-all-done.hidden_ref, bf16[608,512]{1,0:T(8,128)(2,1)S(1)} %kron_factor.1.factor_ref), custom_call_target="tpu_custom_call" | custom-call | flops 1073741824 | bytes 3407872 | tf_op jit(solution)/shard_map/rotate_rows/pallas_call | solution.py:310
  59.1 47.6 %all_to_all.10.packed_ref = bf16[16,424,128]{2,1,0:T(8,128)(2,1)S(1)} all-to-all(bf16[16,424,128]{2,1,0:T(8,128)(2,1)S(1)} %rotate_rows.1), channel_id=1, replica_groups=mesh['dp'=32,'tensor'=16] {'tensor'}, dimensions={0} | all-to-all | bytes 3473408 | tf_op jit(solution)/shard_map/all_to_all | solution.py:337
  106.7 1.9 %unpack.1 = (bf16[16,16,3328]{2,1,0:T(8,128)(2,1)}, f32[2,128]{1,0:T(2,128)}) custom-call(bf16[16,424,128]{2,1,0:T(8,128)(2,1)S(1)} %all_to_all.10.packed_ref), custom_call_target="tpu_custom_call" | custom-call | tf_op jit(solution)/shard_map/unpack/pallas_call | solution.py:110
Async XLA Ops:
  3.6 11.9 %copy-start = (bf16[52,52]{1,0:T(8,128)(2,1)S(1)}, bf16[52,52]{1,0:T(8,128)(2,1)}, u32[]{:S(2)}) copy-start(bf16[52,52]{1,0:T(8,128)(2,1)} %rotation_ref.1) | copy-start | bytes 16228
  3.7 52.9 %all-to-all-start = ((bf16[16,16,3328]{2,1,0:T(8,128)(2,1)}), bf16[16,16,3328]{2,1,0:T(8,128)(2,1)S(1)}, u32[]{:S(2)}, u32[]{:S(2)}) async-start(bf16[16,16,3328]{2,1,0:T(8,128)(2,1)} %bitcast.4), calls=%async_computation | async-start | bytes 3407872 | tf_op jit(solution)/shard_map/all_to_all | solution.py:336

commit v6 on v5

--- a/solution.py
+++ b/solution.py
@@ -65,6 +65,15 @@
     )(gate, up)
 
 
+def packet_rows(i, rows, tiles):
+    start = i * rows + (8 if i == tiles - 1 else 0)
+    return slice(start, start + rows)
+
+
+def peak_rows(rows, tiles):
+    return slice((tiles - 1) * rows, (tiles - 1) * rows + 8)
+
+
 def unpack_kernel(packed_ref, out_hbm, peak_ref, held_ref, sems):
     groups, rows, width = held_ref.shape
     steps, span = peak_ref.shape
@@ -75,7 +84,7 @@
     for part in range(count):
         for group in range(part * each, part * each + each):
             for i in range(width // LANES):
-                value = packed_ref[group, i * rows : (i + 1) * rows, :]
+                value = packed_ref[group, packet_rows(i, rows, width // LANES), :]
                 held_ref[group, :, i * LANES : (i + 1) * LANES] = value
         at = pl.ds(part * each, each)
         copy = pltpu.make_async_copy(held_ref.at[at], out_hbm.at[at], sems.at[part])
@@ -85,7 +94,7 @@
     def iota(shape, dim):
         return lax.broadcasted_iota(jnp.int32, shape, dim)
 
-    parts = packed_ref[:, width // LANES * rows :, :].astype(f32).reshape(groups * 8, LANES)
+    parts = packed_ref[:, peak_rows(rows, width // LANES), :].astype(f32).reshape(groups * 8, LANES)
     pick = (iota((8, LANES), 0) == iota((8, LANES), 1)).astype(f32).astype(bf16)
     turned = lax.dot_general(
         pick, parts.astype(bf16), (((1,), (1,)), ((), ())), preferred_element_type=f32
@@ -300,8 +309,8 @@
     for group in range(groups):
         for i in range(width // LANES):
             value = rotated_ref[group, :, i * LANES : (i + 1) * LANES] * inverse
-            out_ref[group, i * rows : (i + 1) * rows, :] = value.astype(out_ref.dtype)
-        out_ref[group, width // LANES * rows :, :] = parts
+            out_ref[group, packet_rows(i, rows, width // LANES), :] = value.astype(out_ref.dtype)
+        out_ref[group, peak_rows(rows, width // LANES), :] = parts
 
 
 def transform(hidden, weights):

time: 109 us -> 109 us (level)
  no operation moved by 1% of the time
where the time goes in v6:
time: 109 us
  blocking collectives  47.6 us (44%)
  waiting for transfers between devices  40.4 us (37%)
  starting transfers between devices  11.8 us (11%)
  Pallas kernels  8.19 us (8%)
    all_to_all x1, blocking collectives, body(): packed = lax.all_to_all(transform(mine, weights), 'tensor', 0, 0)  47.6 us
    all_to_all x1, waiting for transfers between devices, body(): mine = lax.all_to_all(hidden.reshape(groups, -1, width), 'tensor', 0, 0)  40.4 us
    all_to_all x1, starting transfers between devices, body(): mine = lax.all_to_all(hidden.reshape(groups, -1, width), 'tensor', 0, 0)  11.8 us
    pallas_call x1, Pallas kernels, gated(): pl.pallas_call(hidden_kernel, out_shape=jax.ShapeDtypeStruct(gate.shape,...  3.01 us
    pallas_call x1, Pallas kernels, transform(): pl.pallas_call(transform_kernel, out_shape=jax.ShapeDtypeStruct((groups,...  2.57 us
  transfers between devices with their start and end apart: 1, of which 1 were waited for; matrix products, arithmetic and copies ran while one was open for 0% of the time, Pallas kernels for 1%

profile of v6, /device:TPU:1, one launch (start us, length us, event | category | flops | bytes accessed | tf_op | source)
XLA Modules:
  0.0 108.6 jit_solution(8323376522126216646)
XLA Ops:
  0.6 3.0 %gated_hidden.1 = bf16[256,3328]{1,0:T(8,128)(2,1)} custom-call(bf16[256,3328]{1,0:T(8,128)(2,1)} %bitcast.5, bf16[256,3328]{1,0:T(8,128)(2,1)} %bitcast.6), custom_call_target="tpu_custom_call" | custom-call | flops 5111808 | bytes 5111808 | tf_op jit(solution)/shard_map/gated_hidden/pallas_call | solution.py:54
  3.6 0.0 copy-start
  3.7 11.8 %all-to-all-start = ((bf16[16,16,3328]{2,1,0:T(8,128)(2,1)}), bf16[16,16,3328]{2,1,0:T(8,128)(2,1)S(1)}, u32[]{:S(2)}, u32[]{:S(2)}) async-start(bf16[16,16,3328]{2,1,0:T(8,128)(2,1)} %bitcast.4), calls=%async_computation | async-start | bytes 3407872 | tf_op jit(solution)/shard_map/all_to_all | solution.py:345
  15.5 0.0 copy-done
  15.5 0.7 kron_factor.1.factor_ref
  16.2 40.4 %all-to-all-done.hidden_ref = bf16[16,16,3328]{2,1,0:T(8,128)(2,1)S(1)} async-done(((bf16[16,16,3328]{2,1,0:T(8,128)(2,1)}), bf16[16,16,3328]{2,1,0:T(8,128)(2,1)S(1)}, u32[]{:S(2)}, u32[]{:S(2)}) %all-to-all-start) | async-done | bytes 1703968 | tf_op jit(solution)/shard_map/all_to_all | solution.py:345
  56.6 2.6 %rotate_rows.1 = bf16[16,424,128]{2,1,0:T(8,128)(2,1)S(1)} custom-call(bf16[16,16,3328]{2,1,0:T(8,128)(2,1)S(1)} %all-to-all-done.hidden_ref, bf16[608,512]{1,0:T(8,128)(2,1)S(1)} %kron_factor.1.factor_ref), custom_call_target="tpu_custom_call" | custom-call | flops 1073741824 | bytes 3407872 | tf_op jit(solution)/shard_map/rotate_rows/pallas_call | solution.py:319
  59.1 47.6 %all_to_all.10.packed_ref = bf16[16,424,128]{2,1,0:T(8,128)(2,1)S(1)} all-to-all(bf16[16,424,128]{2,1,0:T(8,128)(2,1)S(1)} %rotate_rows.1), channel_id=1, replica_groups=mesh['dp'=32,'tensor'=16] {'tensor'}, dimensions={0} | all-to-all | bytes 3473408 | tf_op jit(solution)/shard_map/all_to_all | solution.py:346
  106.7 1.9 %unpack.1 = (bf16[16,16,3328]{2,1,0:T(8,128)(2,1)}, f32[2,128]{1,0:T(2,128)}) custom-call(bf16[16,424,128]{2,1,0:T(8,128)(2,1)S(1)} %all_to_all.10.packed_ref), custom_call_target="tpu_custom_call" | custom-call | tf_op jit(solution)/shard_map/unpack/pallas_call | solution.py:119
Async XLA Ops:
  3.6 11.9 %copy-start = (bf16[52,52]{1,0:T(8,128)(2,1)S(1)}, bf16[52,52]{1,0:T(8,128)(2,1)}, u32[]{:S(2)}) copy-start(bf16[52,52]{1,0:T(8,128)(2,1)} %rotation_ref.1) | copy-start | bytes 16228
  3.7 52.9 %all-to-all-start = ((bf16[16,16,3328]{2,1,0:T(8,128)(2,1)}), bf16[16,16,3328]{2,1,0:T(8,128)(2,1)S(1)}, u32[]{:S(2)}, u32[]{:S(2)}) async-start(bf16[16,16,3328]{2,1,0:T(8,128)(2,1)} %bitcast.4), calls=%async_computation | async-start | bytes 3407872 | tf_op jit(solution)/shard_map/all_to_all | solution.py:345

commit v7 on v6

--- a/solution.py
+++ b/solution.py
@@ -12,13 +12,55 @@
 WINDOW = 512
 SIDE = WINDOW // 2
 VMEM_LIMIT = 20 * 1024 * 1024
-STREAM_LIMIT = 58 * 1024 * 1024
-
-
-def hidden_kernel(gate_hbm, up_hbm, out_hbm, gate_ref, up_ref, out_ref, sems):
+STREAM_LIMIT = 51 * 1024 * 1024
+
+
+def parity_sign(left, right):
+    both = left & right
+    parity = both
+    for level in (1, 2):
+        parity = parity ^ (both >> level)
+    return 1 - 2 * (parity & 1)
+
+
+def write_factor(rotation, out_ref):
+    small = rotation.shape[0]
+    size = LOW * small
+    height, width = out_ref.shape
+    margin = height - width
+    f32, bf16 = jnp.float32, jnp.bfloat16
+
+    def block(index):
+        return (index * 1261) >> 16
+
+    def iota(shape, dim):
+        return lax.broadcasted_iota(jnp.int32, shape, dim)
+
+    def one_where(mask):
+        return mask.astype(f32).astype(bf16)
+
+    shape = (small, width)
+    lane = iota(shape, 1)
+    across = one_where((lane - block(lane) * small == iota(shape, 0)) & (lane < size))
+    tiled = jnp.dot(rotation, across, preferred_element_type=f32).astype(bf16)
+    shape = (height, small)
+    row = iota(shape, 0) - margin
+    inside = (row >= 0) & (row < size)
+    down = one_where((row - block(row) * small == iota(shape, 1)) & inside)
+    value = jnp.dot(down, tiled, preferred_element_type=f32)
+    shape = (height, width)
+    sign = parity_sign(block(iota(shape, 0) - margin), block(iota(shape, 1))).astype(f32)
+    out_ref[...] = (value * sign).astype(bf16)
+
+
+def hidden_kernel(
+    gate_hbm, up_hbm, rotation_hbm, out_ref, factor_ref, gate_ref, up_ref, rotation_ref, sems, own_sem
+):
     chunks, rows, width = gate_ref.shape
     f32 = jnp.float32
     block = 32
+    own = pltpu.make_async_copy(rotation_hbm, rotation_ref, own_sem)
+    own.start()
     copies = []
     for chunk in range(chunks):
         at = pl.ds(chunk * rows, rows)
@@ -26,7 +68,8 @@
             copy = pltpu.make_async_copy(source.at[at], target.at[chunk], sems.at[chunk, k])
             copy.start()
             copies.append(copy)
-    results = []
+    own.wait()
+    write_factor(rotation_ref[...], factor_ref)
     for chunk in range(chunks):
         copies[2 * chunk].wait()
         copies[2 * chunk + 1].wait()
@@ -37,32 +80,39 @@
             gate = gate_ref[chunk, at].astype(f32)
             half = 0.5 * gate
             silu = half * jnp.tanh(half) + half
-            out_ref[chunk, at] = (silu * up_ref[chunk, at].astype(f32)).astype(out_ref.dtype)
-
-        at = pl.ds(chunk * rows, rows)
-        result = pltpu.make_async_copy(out_ref.at[chunk], out_hbm.at[at], sems.at[chunk, 2])
-        result.start()
-        results.append(result)
-    for result in results:
-        result.wait()
-
-
-def gated(gate, up):
+            value = (silu * up_ref[chunk, at].astype(f32)).astype(out_ref.dtype)
+            each = out_ref.shape[1]
+            into = pl.ds(chunk * (rows // each) + step * (block // each), block // each)
+            out_ref[into] = value.reshape(block // each, each, width)
+
+
+def gated(gate, up, rotation52, groups):
     rows, width = gate.shape
+    small = rotation52.shape[0]
+    margin = WINDOW - LOW * small
     chunks = 4
     held = pltpu.VMEM((chunks, rows // chunks, width), gate.dtype)
     return pl.pallas_call(
         hidden_kernel,
-        out_shape=jax.ShapeDtypeStruct(gate.shape, gate.dtype),
-        in_specs=[pl.BlockSpec(memory_space=pl.ANY)] * 2,
-        out_specs=pl.BlockSpec(memory_space=pl.ANY),
-        scratch_shapes=[held, held, held, pltpu.SemaphoreType.DMA((chunks, 3))],
+        out_shape=(
+            jax.ShapeDtypeStruct((groups, rows // groups, width), gate.dtype),
+            jax.ShapeDtypeStruct((margin + WINDOW, WINDOW), jnp.bfloat16),
+        ),
+        in_specs=[pl.BlockSpec(memory_space=pl.ANY)] * 3,
+        out_specs=[pl.BlockSpec(memory_space=pltpu.VMEM)] * 2,
+        scratch_shapes=[
+            held,
+            held,
+            pltpu.VMEM((small, small), rotation52.dtype),
+            pltpu.SemaphoreType.DMA((chunks, 2)),
+            pltpu.SemaphoreType.DMA,
+        ],
         compiler_params=pltpu.CompilerParams(vmem_limit_bytes=STREAM_LIMIT),
         cost_estimate=pl.CostEstimate(
             flops=6 * rows * width, bytes_accessed=6 * rows * width, transcendentals=rows * width
         ),
         name="gated_hidden",
-    )(gate, up)
+    )(gate, up, rotation52)
 
 
 def packet_rows(i, rows, tiles):
@@ -129,62 +179,6 @@
         name="unpack",
     )(packed)
     return quantized.reshape(steps, span, width), peaks
-
-
-def parity_sign(left, right):
-    both = left & right
-    parity = both
-    for level in (1, 2):
-        parity = parity ^ (both >> level)
-    return 1 - 2 * (parity & 1)
-
-
-def factor_kernel(rotation_ref, out_ref):
-    small = rotation_ref.shape[0]
-    size = LOW * small
-    height, width = out_ref.shape
-    margin = height - width
-    f32, bf16 = jnp.float32, jnp.bfloat16
-
-    def block(index):
-        return (index * 1261) >> 16
-
-    def iota(shape, dim):
-        return lax.broadcasted_iota(jnp.int32, shape, dim)
-
-    def one_where(mask):
-        return mask.astype(f32).astype(bf16)
-
-    shape = (small, width)
-    lane = iota(shape, 1)
-    across = one_where((lane - block(lane) * small == iota(shape, 0)) & (lane < size))
-    tiled = jnp.dot(rotation_ref[...], across, preferred_element_type=f32).astype(bf16)
-    shape = (height, small)
-    row = iota(shape, 0) - margin
-    inside = (row >= 0) & (row < size)
-    down = one_where((row - block(row) * small == iota(shape, 1)) & inside)
-    value = jnp.dot(down, tiled, preferred_element_type=f32)
-    shape = (height, width)
-    sign = parity_sign(block(iota(shape, 0) - margin), block(iota(shape, 1))).astype(f32)
-    out_ref[...] = (value * sign).astype(bf16)
-
-
-def factor(rotation52):
-    small = rotation52.shape[0]
-    margin = WINDOW - LOW * small
-    return pl.pallas_call(
-        factor_kernel,
-        out_shape=jax.ShapeDtypeStruct((margin + WINDOW, WINDOW), jnp.bfloat16),
-        in_specs=[pl.BlockSpec(memory_space=pltpu.VMEM)],
-        out_specs=pl.BlockSpec(memory_space=pltpu.VMEM),
-        compiler_params=pltpu.CompilerParams(vmem_limit_bytes=VMEM_LIMIT),
-        cost_estimate=pl.CostEstimate(
-            flops=2 * (margin + WINDOW) * WINDOW * small,
-            bytes_accessed=2 * (margin + WINDOW) * WINDOW,
-            transcendentals=0,
-        ),
-        name="kron_factor",
-    )(rotation52)
 
 
 def butterfly(values):
@@ -339,10 +333,9 @@
 def body(gate_pre, up_pre, rotation52):
     steps, rows, width = gate_pre.shape
     groups = lax.axis_size("tensor")
-    weights = factor(rotation52)
     flat = (steps * rows, width)
-    hidden = gated(gate_pre.reshape(flat), up_pre.reshape(flat))
-    mine = lax.all_to_all(hidden.reshape(groups, -1, width), "tensor", 0, 0)
+    hidden, weights = gated(gate_pre.reshape(flat), up_pre.reshape(flat), rotation52, groups)
+    mine = lax.all_to_all(hidden, "tensor", 0, 0)
     packed = lax.all_to_all(transform(mine, weights), "tensor", 0, 0)
     return unpack(packed, steps, rows, width)
 

time: 109 us -> 109 us (level)
  blocking collectives: 47.6 us -> 100 us
  waiting for transfers between devices: 40.4 us -> 0 us
  starting transfers between devices: 11.8 us -> 0 us
  Pallas kernels: 8.19 us -> 6.74 us
    all_to_all x0 -> x1, blocking collectives: none -> 54.3 us  [body(): mine = lax.all_to_all(hidden, 'tensor', 0, 0)]
    all_to_all x1 -> x0, waiting for transfers between devices: 40.4 us -> none  [body(): mine = lax.all_to_all(hidden.reshape(groups, -1, width), 'tensor', 0, 0)]
    all_to_all x1 -> x0, starting transfers between devices: 11.8 us -> none  [body(): mine = lax.all_to_all(hidden.reshape(groups, -1, width), 'tensor', 0, 0)]
    all_to_all x1, blocking collectives: 47.6 us -> 45.9 us  [body(): packed = lax.all_to_all(transform(mine, weights), 'tensor', 0, 0)]
    pallas_call x2 -> x1, Pallas kernels: 3.68 us -> 2.23 us  [gated(): pl.pallas_call(hidden_kernel, out_shape=(jax.ShapeDtypeStruct((groups, ro...]
  transfers between devices with their start and end apart: 1 -> 0, of which waited for: 1 -> 0; matrix products, arithmetic and copies ran while one was open for 0% -> 0% of each run, Pallas kernels for 1% -> 0%
where the time goes in v7:
time: 109 us; the launch traced here: 108 us
  blocking collectives  100 us (92%)
  Pallas kernels  6.74 us (6%)
    all_to_all x1, blocking collectives, body(): mine = lax.all_to_all(hidden, 'tensor', 0, 0)  54.3 us
    all_to_all x1, blocking collectives, body(): packed = lax.all_to_all(transform(mine, weights), 'tensor', 0, 0)  45.9 us
    pallas_call x1, Pallas kernels, transform(): pl.pallas_call(transform_kernel, out_shape=jax.ShapeDtypeStruct((groups,...  2.57 us
    pallas_call x1, Pallas kernels, gated(): pl.pallas_call(hidden_kernel, out_shape=(jax.ShapeDtypeStruct((groups, ro...  2.23 us

profile of v7, /device:TPU:1, one launch (start us, length us, event | category | flops | bytes accessed | tf_op | source)
XLA Modules:
  0.0 108.4 jit_solution(7515194157514381684)
XLA Ops:
  0.6 0.0 copy-start
  0.6 0.7 copy-done
  1.3 2.2 %gated_hidden.1 = (bf16[16,16,3328]{2,1,0:T(8,128)(2,1)S(1)}, bf16[608,512]{1,0:T(8,128)(2,1)S(1)}) custom-call(bf16[256,3328]{1,0:T(8,128)(2,1)} %bitcast.3, bf16[256,3328]{1,0:T(8,128)(2,1)} %bitcast.4, bf16[52,52]{1,0:T(8,128)(2,1)S(1)} %copy-done), custom_call_target="tpu_custom_call" | custom-call | flops 5111808 | bytes 5111808 | tf_op jit(solution)/shard_map/gated_hidden/pallas_call | solution.py:95
  3.6 54.3 %all_to_all.10.hidden_ref = bf16[16,16,3328]{2,1,0:T(8,128)(2,1)S(1)} all-to-all(bf16[16,16,3328]{2,1,0:T(8,128)(2,1)S(1)} %get-tuple-element.6), channel_id=1, replica_groups=mesh['dp'=32,'tensor'=16] {'tensor'}, dimensions={0} | all-to-all | bytes 3407872 | tf_op jit(solution)/shard_map/all_to_all | solution.py:338
  57.9 2.6 %rotate_rows.1 = bf16[16,424,128]{2,1,0:T(8,128)(2,1)S(1)} custom-call(bf16[16,16,3328]{2,1,0:T(8,128)(2,1)S(1)} %all_to_all.10.hidden_ref, bf16[608,512]{1,0:T(8,128)(2,1)S(1)} %get-tuple-element.7.factor_ref), custom_call_target="tpu_custom_call" | custom-call | flops 1073741824 | bytes 3407872 | tf_op jit(solution)/shard_map/rotate_rows/pallas_call | solution.py:313
  60.5 45.9 %all_to_all.11.packed_ref = bf16[16,424,128]{2,1,0:T(8,128)(2,1)S(1)} all-to-all(bf16[16,424,128]{2,1,0:T(8,128)(2,1)S(1)} %rotate_rows.1), channel_id=1, replica_groups=mesh['dp'=32,'tensor'=16] {'tensor'}, dimensions={0} | all-to-all | bytes 3473408 | tf_op jit(solution)/shard_map/all_to_all | solution.py:339
  106.4 1.9 %unpack.1 = (bf16[16,16,3328]{2,1,0:T(8,128)(2,1)}, f32[2,128]{1,0:T(2,128)}) custom-call(bf16[16,424,128]{2,1,0:T(8,128)(2,1)S(1)} %all_to_all.11.packed_ref), custom_call_target="tpu_custom_call" | custom-call | tf_op jit(solution)/shard_map/unpack/pallas_call | solution.py:169
Async XLA Ops:
  0.6 0.7 copy-start
